TPU v7x, 256 devices: a whole 4x4x8 slice. The times are simulated.
256 devices in a mesh: view: 64 (over z, y, core), head: 4 (over x).
Axes of the slice: x: 4, y: 4, z: 8, core: 2. Of those that a mesh axis runs over, the one named last changes fastest.
Arguments:
- inputs: bfloat16 [64, 128, 1280], P('view', None, 'head'), may hold values from -6 to 6
- output_gradient: bfloat16 [64, 128, 1280], P('view', None, 'head'), may hold values from -6 to 6
- query_key_value_weight: bfloat16 [3, 1280, 1280], P(None, None, 'head'), may hold values from -0.15625 to 0.15625
- output_weight: bfloat16 [1280, 1280], P('head'), may hold values from -0.15625 to 0.15625
- adapter_down_maps: bfloat16 [3, 1280, 64], replicated, may hold values from -0.15625 to 0.15625
- adapter_up_maps: bfloat16 [3, 64, 1280], P(None, None, 'head'), may hold values from -0.75 to 0.75
- adjacent: int32 [64, 64], P('view'), may hold values from 0 to 1, as said below
Outputs:
- layer_out: bfloat16 [64, 128, 1280], P('view', None, 'head')
- grad_inputs: bfloat16 [64, 128, 1280], P('view', None, 'head')
- grad_a: float32 [3, 1280, 64], P(None, 'head')
- grad_b: float32 [3, 64, 1280], P(None, None, 'head')
Inputs may be any that keep to these rules, and one draw needn't show every extreme that they name: adjacent[i, i] is 1; adjacent[i, j] can be 1 only when the circular distance between i and j is at most 8; each row holds at most 16 ones off the diagonal and at least 4 of them; some row holds the most and some row the least.
All inputs are finite; a program needn't handle non-finite values.
Results may differ from a plain program's by a relative error of at most 0.024.
Values may be sent and summed in bfloat16 or wider, within the bound.
A program may use at most 64 MiB of HBM per device.

v0:
```python
import jax
import jax.numpy as jnp
from jax import lax
from jax.experimental import pallas as pl
from jax.experimental.pallas import tpu as pltpu
from jax.sharding import PartitionSpec as P

MESH = pl.DeviceIdType.MESH
F32 = jnp.float32
BF16 = jnp.bfloat16
T = 128
W = 320
D = 64
R = 64
CHIPS = 32
ROWS = 48


def mm(a, b):
    return lax.dot_general(a, b, (((1,), (0,)), ((), ())), preferred_element_type=F32)


def mm_nt(a, b):
    return lax.dot_general(a, b, (((1,), (1,)), ((), ())), preferred_element_type=F32)


def kernel(
    x_ref, og_ref, adj_ref, wqkv_hbm, wo_hbm, down_hbm, up_hbm,
    lo_ref, gi_ref, ga_ref, gb_ref,
    wqkv, wo, down, up, wsem,
    xs, ogs, xfull, ogfull, xsend, xrecv, ogsend, ogrecv,
    kv, qg, kvsend, kvrecv, kvbsend, kvbrecv, qgsend, qgrecv, qgbsend, qgbrecv,
    st, stown, stsend, strecv,
    aq, ag, a4q, a4g, ak, av, a4kv, wtab,
    est, est4, oacc, o4acc, invb, delb, inv4, del4, dq, dq4, dk, dv, dkv4,
    att, gs, low, inacc, losrc, lobuf, losend, lorecv,
    lgsrc, lgbuf, lgsend, lgrecv, gisrc, gibuf, gisend, girecv,
    acc, accb, rsbuf, rssend, rsrecv, zbuf, zsend, zrecv, fin, finsend, finrecv,
):
    view = lax.axis_index("view")
    head = lax.axis_index("head")
    chip = view // 2
    core = lax.rem(view, 2)
    z = view // 8
    spot = lax.rem(view, 8)
    sgn = 2 * core - 1

    def at(c, k):
        return (lax.rem(c + 2 * CHIPS, CHIPS) * 2 + k, head)

    def step(p, side):
        near = ((p + 1) // 2) * (2 * lax.rem(p, 2) - 1)
        if isinstance(p, int):
            return {7: 4 * side, 8: -4 * side}.get(p, near)
        return jnp.where(p == 7, 4 * side, jnp.where(p == 8, -4 * side, near))

    sibling = (chip * 2 + 1 - core, head)

    def z_peer(o):
        return (lax.rem(z + o, 8) * 8 + spot, head)

    def spot_peer(o):
        return (z * 8 + lax.rem(spot + o, 8), head)

    def x_peer(o):
        return (view, lax.rem(head + o, 4))

    def remote(src, dst, ss, rs, dev):
        return pltpu.make_async_remote_copy(
            src_ref=src, dst_ref=dst, send_sem=ss, recv_sem=rs,
            device_id=dev, device_id_type=MESH,
        )

    weights = [
        pltpu.make_async_copy(s, d, wsem.at[i])
        for i, (s, d) in enumerate(
            ((wqkv_hbm, wqkv), (down_hbm, down), (up_hbm, up), (wo_hbm, wo))
        )
    ]
    for w in weights:
        w.start()

    barrier = pltpu.get_barrier_semaphore()

    def greet(dev):
        pl.semaphore_signal(barrier, inc=1, device_id=dev, device_id_type=MESH)

    for o in (1, 2, 3):
        greet(x_peer(o))

    @pl.loop(1, 9)
    def _(o):
        greet((lax.rem(view + o, 64), head))
        greet((lax.rem(view + 64 - o, 64), head))

    for o in (2, 3, 4, 5, 6):
        greet(z_peer(o))
    pl.semaphore_wait(barrier, 24)

    def x_copy(o):
        return remote(x_ref.at[0], xs.at[head], xsend.at[o], xrecv.at[o], x_peer(o))

    def og_copy(o):
        return remote(og_ref.at[0], ogs.at[head], ogsend.at[o], ogrecv.at[o], x_peer(o))

    for o in (1, 3, 2):
        x_copy(o).start()
    for o in (1, 3, 2):
        og_copy(o).start()
    xs[head] = x_ref[0]
    ogs[head] = og_ref[0]

    adj = adj_ref[...].astype(F32)
    lane64 = lax.broadcasted_iota(jnp.int32, (1, 64), 1)

    def weight_of(v):
        one = jnp.sum(jnp.where(lane64 == v, adj, 0.0), axis=1, keepdims=True)
        return jnp.broadcast_to(one, (1, T))

    for p in range(9):
        c = lax.rem(chip + step(p, sgn) + 2 * CHIPS, CHIPS) * 2
        wtab[p : p + 1, 0:T] = weight_of(c + core)
        wtab[p : p + 1, T : 2 * T] = weight_of(c + 1 - core)
    lane = lax.broadcasted_iota(jnp.int32, (T, T), 1)
    left = lane < D

    def block_diagonal(dst, i, tile):
        zero = jnp.zeros_like(tile)
        dst[i, 0:T, :] = jnp.where(left, tile, zero)
        dst[i, T : 2 * T, :] = jnp.where(left, zero, tile)

    for w in weights[:3]:
        w.wait()
    for o in (1, 2, 3):
        x_copy(o).wait_recv()
    for h in range(4):
        xfull[:, W * h : W * (h + 1)] = xs[h]
    rows = xfull[...]

    def project(m):
        low_m = mm(rows, down[m]).astype(BF16)
        low[m] = low_m
        return (mm(rows, wqkv[m]) + 0.5 * mm(low_m, up[m])).astype(BF16)

    key = project(1)
    value = project(2)
    kv[0:T, 0:256] = key[:, 0:256]
    kv[0:T, 256:512] = value[:, 0:256]
    kv[0:T, 512:576] = key[:, 256:320]
    kv[0:T, 576:640] = value[:, 256:320]

    def pair_rows(p):
        return pl.ds(pl.multiple_of(p * 256, 256), T)

    def sib_rows(p):
        return pl.ds(pl.multiple_of(p * 256 + T, T), T)

    def block_copy(buf, ss, rs, p):
        return remote(
            buf.at[0:T], buf.at[pair_rows(p)], ss.at[p], rs.at[p],
            at(chip - step(p, sgn), core),
        )

    def sib_copy(buf, ss, rs, p, into):
        return remote(
            buf.at[pair_rows(p)], buf.at[sib_rows(into)], ss.at[into], rs.at[into], sibling
        )

    def kv_copy(p):
        return block_copy(kv, kvsend, kvrecv, p)

    def kvb_copy(p, into):
        return sib_copy(kv, kvbsend, kvbrecv, p, into)

    def qg_copy(p):
        return block_copy(qg, qgsend, qgrecv, p)

    def qgb_copy(p, into):
        return sib_copy(qg, qgbsend, qgbrecv, p, into)

    kvb_copy(0, 0).start()

    @pl.loop(1, 9)
    def _(p):
        kv_copy(p).start()

    query = project(0)
    qg[0:T, 0:256] = query[:, 0:256]
    qg[0:T, 512:576] = query[:, 256:320]

    weights[3].wait()
    for o in (1, 2, 3):
        og_copy(o).wait_recv()
    for h in range(4):
        ogfull[:, W * h : W * (h + 1)] = ogs[h]
    grad_att = mm_nt(ogfull[...], wo[...]).astype(BF16)
    qg[0:T, 256:512] = grad_att[:, 0:256]
    qg[0:T, 576:640] = grad_att[:, 256:320]
    qgb_copy(0, 0).start()

    @pl.loop(1, 9)
    def _(p):
        qg_copy(p).start()

    eighth = jnp.asarray(0.125, BF16)
    for i in range(2):
        block_diagonal(aq, i, qg[0:T, T * i : T * (i + 1)] * eighth)
        block_diagonal(ag, i, qg[0:T, 256 + T * i : 256 + T * (i + 1)])
        block_diagonal(ak, i, kv[0:T, T * i : T * (i + 1)] * eighth)
        block_diagonal(av, i, kv[0:T, 256 + T * i : 256 + T * (i + 1)])
    tile = qg[0:T, 512:640]
    a4q[...] = jnp.where(left, tile * eighth, jnp.zeros_like(tile))
    a4g[...] = jnp.where(left, jnp.zeros_like(tile), tile)
    tile = kv[0:T, 512:640]
    a4kv[0:T, :] = jnp.where(left, tile * eighth, jnp.zeros_like(tile))
    a4kv[T : 2 * T, :] = jnp.where(left, jnp.zeros_like(tile), tile)

    oacc[...] = jnp.zeros_like(oacc)
    o4acc[...] = jnp.zeros_like(o4acc)
    dq[...] = jnp.zeros_like(dq)
    dq4[...] = jnp.zeros_like(dq4)
    dk[...] = jnp.zeros_like(dk)
    dv[...] = jnp.zeros_like(dv)
    dkv4[...] = jnp.zeros_like(dkv4)

    def block(buf, p, n):
        span = pl.ds(pl.multiple_of(p * 256, 256), n)
        return [buf[span, T * i : T * (i + 1)] for i in range(5)]

    def forward(p, n):
        k0, k1, v0, v1, kv4 = block(kv, p, n)
        weight = wtab[pl.ds(p, 1), 0:n]
        ones = jnp.ones((n, T), BF16)
        for i, (k, v) in enumerate(((k0, v0), (k1, v1))):
            e = (jnp.exp(mm_nt(aq[i], k)) * weight).astype(BF16)
            est[p, i, :, 0:n] = e
            oacc[i] += mm(e, jnp.concatenate([v, ones], axis=1))
        e = (jnp.exp(mm_nt(a4q[...], kv4)) * weight).astype(BF16)
        est4[p, :, 0:n] = e
        o4acc[...] += mm(e, jnp.concatenate([kv4, ones], axis=1))

    @pl.loop(1, 7)
    def _(p):
        kv_copy(p).wait_recv()
        kvb_copy(p, p).start()
        kvb_copy(p - 1, p - 1).wait_recv()
        forward(p - 1, 256)

    kv_copy(8).wait_recv()
    kvb_copy(8, 7).start()
    kvb_copy(6, 6).wait_recv()
    forward(6, 256)
    forward(8, T)
    kv_copy(7).wait_recv()
    kvb_copy(8, 7).wait_recv()
    forward(7, 256)

    def diagonal(a):
        return jnp.where(left, a[0:T], a[T : 2 * T])

    stats = jnp.zeros((T, T), F32)

    def put(stats, i, column):
        return jnp.where(lane == i, column, stats)

    for i in range(2):
        inv = 1.0 / oacc[i, :, T : 2 * T]
        invb[i] = inv
        pair = diagonal(oacc[i, :, 0:T] * inv).astype(BF16)
        att[:, T * i : T * (i + 1)] = pair
        prod = pair.astype(F32) * qg[0:T, 256 + T * i : 256 + T * (i + 1)].astype(F32)
        first = jnp.sum(jnp.where(left, prod, 0.0), axis=1, keepdims=True)
        second = jnp.sum(jnp.where(left, 0.0, prod), axis=1, keepdims=True)
        delb[i, 0:T, :] = jnp.broadcast_to(first, (T, T))
        delb[i, T : 2 * T, :] = jnp.broadcast_to(second, (T, T))
        stats = put(stats, 2 * i, inv[0:T])
        stats = put(stats, 2 * i + 1, inv[T : 2 * T])
        stats = put(stats, 5 + 2 * i, first)
        stats = put(stats, 6 + 2 * i, second)
    inv = 1.0 / o4acc[:, T : 2 * T]
    inv4[...] = inv
    last = (o4acc[:, 0:T] * inv).astype(BF16)
    att[:, 256:320] = last[:, D:T]
    prod = last.astype(F32) * qg[0:T, 512:640].astype(F32)
    first = jnp.sum(jnp.where(left, 0.0, prod), axis=1, keepdims=True)
    del4[...] = jnp.broadcast_to(first, (T, T))
    stats = put(stats, 4, inv)
    stats = put(stats, 9, first)
    stown[...] = jnp.transpose(stats)[0:16, :]
    stown[10:11, 0:64] = adj

    def st_copy(p):
        return remote(
            stown, st.at[p, 0], stsend.at[p, 0], strecv.at[p, 0],
            at(chip - step(p, sgn), core),
        )

    def stb_copy(p):
        return remote(
            stown, st.at[p, 1], stsend.at[p, 1], strecv.at[p, 1],
            at(chip - step(p, -sgn), 1 - core),
        )

    @pl.loop(0, 8)
    def _(p):
        st_copy(p + 1).start()
        stb_copy(p).start()

    st[0, 0] = stown[...]

    share = mm(att[...], wo[...]).astype(BF16)
    for h in range(4):
        losrc[h] = share[:, W * h : W * (h + 1)]

    def lo_copy(o):
        return remote(
            losrc.at[lax.rem(head + o, 4)], lobuf.at[o], losend.at[o], lorecv.at[o], x_peer(o)
        )

    for o in (1, 2, 3):
        lo_copy(o).start()

    def wide(a, n):
        return a if n == T else jnp.concatenate([a, a], axis=1)

    def backward_q(p, n):
        k0, k1, v0, v1, kv4 = block(kv, p, n)
        for i, (k, v) in enumerate(((k0, v0), (k1, v1))):
            prob = est[p, i, :, 0:n].astype(F32) * wide(invb[i], n)
            dl = prob * (mm_nt(ag[i], v) - wide(delb[i], n))
            dq[i] += mm(dl.astype(BF16), k)
        prob = est4[p, :, 0:n].astype(F32) * wide(inv4[...], n)
        dl = prob * (mm_nt(a4g[...], kv4) - wide(del4[...], n))
        dq4[...] += mm(dl.astype(BF16), kv4)

    backward_q(0, 256)

    @pl.loop(1, 7)
    def _(p):
        qg_copy(p).wait_recv()
        qgb_copy(p, p).start()
        backward_q(p, 256)

    qg_copy(8).wait_recv()
    qgb_copy(8, 7).start()
    backward_q(7, 256)
    backward_q(8, T)
    for i in range(2):
        gs[0, :, T * i : T * (i + 1)] = (diagonal(dq[i]) * 0.125).astype(BF16)
    gs[0, :, 256:320] = (dq4[:, 0:D] * 0.125).astype(BF16)
    inacc[...] = mm_nt(gs[0], wqkv[0])

    me_lane = lax.broadcasted_iota(jnp.int32, (1, T), 1) == view

    def backward_kv(p, n):
        q0, q1, g0, g1, qg4 = block(qg, p, n)
        sides = [st[p, s] for s in range(n // T)]
        invs, deltas = [], []
        for s in sides:
            w = jnp.sum(jnp.where(me_lane, s[10:11, :], 0.0), axis=1, keepdims=True)
            invs.append(s * w)
        invs = invs[0] if n == T else jnp.concatenate(invs, axis=1)
        deltas = sides[0] if n == T else jnp.concatenate(sides, axis=1)

        def weigh(e, h):
            return e * invs[h : h + 1, :]

        def shift(dp, h):
            return dp - deltas[5 + h : 6 + h, :]

        for i, (q, g) in enumerate(((q0, g0), (q1, g1))):
            e = jnp.exp(mm_nt(ak[i], q))
            dp = mm_nt(av[i], g)
            prob = [weigh(e[0:T], 2 * i), weigh(e[T : 2 * T], 2 * i + 1)]
            dl = [prob[0] * shift(dp[0:T], 2 * i), prob[1] * shift(dp[T : 2 * T], 2 * i + 1)]
            prob = jnp.concatenate(prob, axis=0).astype(BF16)
            dl = jnp.concatenate(dl, axis=0).astype(BF16)
            dk[i] += mm(dl, q)
            dv[i] += mm(prob, g)
        both = mm_nt(a4kv[...], qg4)
        prob = weigh(jnp.exp(both[0:T]), 4)
        dl = prob * shift(both[T : 2 * T], 4)
        dkv4[...] += mm(jnp.concatenate([dl, prob], axis=0).astype(BF16), qg4)

    def st_wait(p):
        st_copy(p).wait_recv()

    stb_copy(0).wait_recv()
    qgb_copy(0, 0).wait_recv()
    backward_kv(0, 256)

    @pl.loop(1, 7)
    def _(p):
        qgb_copy(p, p).wait_recv()
        st_copy(p).wait_recv()
        stb_copy(p).wait_recv()
        backward_kv(p, 256)

    st_copy(8).wait_recv()
    backward_kv(8, T)
    st_copy(7).wait_recv()
    stb_copy(7).wait_recv()
    qg_copy(7).wait_recv()
    qgb_copy(8, 7).wait_recv()
    backward_kv(7, 256)

    for i in range(2):
        gs[1, :, T * i : T * (i + 1)] = (diagonal(dk[i]) * 0.125).astype(BF16)
        gs[2, :, T * i : T * (i + 1)] = diagonal(dv[i]).astype(BF16)
    gs[1, :, 256:320] = (dkv4[0:T, 0:D] * 0.125).astype(BF16)
    gs[2, :, 256:320] = dkv4[T : 2 * T, D:T].astype(BF16)

    for m in range(3):
        lgsrc[R * m : R * (m + 1), :] = (0.5 * mm_nt(up[m], gs[m])).astype(BF16)

    def lg_copy(o):
        return remote(lgsrc, lgbuf.at[o], lgsend.at[o], lgrecv.at[o], x_peer(o))

    for o in (1, 2, 3):
        lg_copy(o).start()

    share = (inacc[...] + mm_nt(gs[1], wqkv[1]) + mm_nt(gs[2], wqkv[2])).astype(BF16)
    for h in range(4):
        gisrc[h] = share[:, W * h : W * (h + 1)]

    def gi_copy(o):
        return remote(
            gisrc.at[lax.rem(head + o, 4)], gibuf.at[o], gisend.at[o], girecv.at[o], x_peer(o)
        )

    for o in (1, 2, 3):
        gi_copy(o).start()
    for m in range(3):
        acc[3 * R + R * m : 3 * R + R * (m + 1), :] = 0.5 * mm(
            jnp.transpose(low[m].astype(F32)).astype(BF16), gs[m]
        )

    for o in (1, 2, 3):
        lg_copy(o).wait_recv()
    lg = lgsrc[...].astype(F32)
    for o in (1, 2, 3):
        lg = lg + lgbuf[o].astype(F32)
    lg = lg.astype(BF16)
    for m in range(3):
        acc[R * m : R * (m + 1), :] = mm(lg[R * m : R * (m + 1), :], x_ref[0])

    accb[...] = acc[...].astype(BF16)

    def share_rows(i):
        return pl.ds(pl.multiple_of(i * ROWS, 16), ROWS)

    def rs_copy(o):
        return remote(
            accb.at[share_rows(lax.rem(spot + o, 8))], rsbuf.at[o],
            rssend.at[o], rsrecv.at[o], spot_peer(o),
        )

    for o in range(1, 8):
        rs_copy(o).start()

    own = jnp.zeros((T, W), F32)
    lgt = jnp.transpose(lg.astype(F32)).astype(BF16)
    for m in range(3):
        part = down[m, pl.ds(pl.multiple_of(head * W, 64), W), :]
        own = own + mm_nt(lgt[:, R * m : R * (m + 1)], part)
    own = own + gisrc[head].astype(F32)
    for o in (1, 2, 3):
        gi_copy(o).wait_recv()
        own = own + gibuf[o].astype(F32)
    gi_ref[0] = own.astype(BF16)
    out = losrc[head].astype(F32)
    for o in (1, 2, 3):
        lo_copy(o).wait_recv()
        out = out + lobuf[o].astype(F32)
    lo_ref[0] = out.astype(BF16)

    total = acc[share_rows(spot), :]
    for o in range(1, 8):
        rs_copy(o).wait_recv()
        total = total + rsbuf[o].astype(F32)
    zbuf[z] = total.astype(BF16)

    def z_copy(o):
        return remote(zbuf.at[z], zbuf.at[z], zsend.at[o], zrecv.at[o], z_peer(o))

    for o in range(1, 8):
        z_copy(o).start()
    for o in range(1, 8):
        z_copy(o).wait_recv()
    total = zbuf[0].astype(F32)
    for i in range(1, 8):
        total = total + zbuf[i].astype(F32)
    fin[spot] = total.astype(BF16)

    def fin_copy(o):
        return remote(fin.at[spot], fin.at[spot], finsend.at[o], finrecv.at[o], spot_peer(o))

    for o in range(1, 8):
        fin_copy(o).start()
    for o in range(1, 8):
        fin_copy(o).wait_recv()
    for i in range(4):
        first = i * ROWS
        for r in range(0, ROWS, 16):
            m, at_row = divmod(first + r, R)
            ga_ref[m, at_row : at_row + 16, :] = fin[i, r : r + 16, :].astype(F32)
            gb_ref[m, at_row : at_row + 16, :] = fin[i + 4, r : r + 16, :].astype(F32)

    for o in (1, 2, 3):
        x_copy(o).wait_send()
        og_copy(o).wait_send()
        lo_copy(o).wait_send()
        lg_copy(o).wait_send()
        gi_copy(o).wait_send()

    @pl.loop(1, 9)
    def _(p):
        kv_copy(p).wait_send()
        qg_copy(p).wait_send()
        st_copy(p).wait_send()
        stb_copy(p - 1).wait_send()

    @pl.loop(0, 7)
    def _(p):
        kvb_copy(p, p).wait_send()
        qgb_copy(p, p).wait_send()

    kvb_copy(8, 7).wait_send()
    qgb_copy(8, 7).wait_send()
    for o in range(1, 8):
        rs_copy(o).wait_send()
        z_copy(o).wait_send()
        fin_copy(o).wait_send()


def body(inputs, output_gradient, wqkv, wo, down, up, adjacent):
    vmem = pltpu.VMEM
    dma = pltpu.SemaphoreType.DMA
    scratch = [
        vmem((3, 1280, W), BF16), vmem((W, 1280), BF16), vmem((3, 1280, R), BF16),
        vmem((3, R, W), BF16), dma((4,)),
        vmem((4, T, W), BF16), vmem((4, T, W), BF16), vmem((T, 1280), BF16),
        vmem((T, 1280), BF16), dma((4,)), dma((4,)), dma((4,)), dma((4,)),
        vmem((17 * T, 640), BF16), vmem((17 * T, 640), BF16),
        dma((9,)), dma((9,)), dma((8,)), dma((8,)), dma((9,)), dma((9,)), dma((8,)), dma((8,)),
        vmem((9, 2, 16, T), F32), vmem((16, T), F32), dma((9, 2)), dma((9, 2)),
        vmem((2, 256, T), BF16), vmem((2, 256, T), BF16), vmem((T, T), BF16), vmem((T, T), BF16),
        vmem((2, 256, T), BF16), vmem((2, 256, T), BF16), vmem((256, T), BF16),
        vmem((16, 256), F32),
        vmem((9, 2, 256, 256), BF16), vmem((9, T, 256), BF16), vmem((2, 256, 256), F32),
        vmem((T, 256), F32), vmem((2, 256, T), F32), vmem((2, 256, T), F32), vmem((T, T), F32),
        vmem((T, T), F32), vmem((2, 256, T), F32), vmem((T, T), F32), vmem((2, 256, T), F32),
        vmem((2, 256, T), F32), vmem((256, T), F32),
        vmem((T, W), BF16), vmem((3, T, W), BF16), vmem((3, T, R), BF16), vmem((T, 1280), F32),
        vmem((4, T, W), BF16), vmem((4, T, W), BF16), dma((4,)), dma((4,)),
        vmem((3 * R, T), BF16), vmem((4, 3 * R, T), BF16), dma((4,)), dma((4,)),
        vmem((4, T, W), BF16), vmem((4, T, W), BF16), dma((4,)), dma((4,)),
        vmem((6 * R, W), F32), vmem((6 * R, W), BF16), vmem((8, ROWS, W), BF16), dma((8,)),
        dma((8,)), vmem((8, ROWS, W), BF16), dma((8,)), dma((8,)), vmem((8, ROWS, W), BF16),
        dma((8,)), dma((8,)),
    ]
    whole = pl.BlockSpec(memory_space=pltpu.VMEM)
    anywhere = pl.BlockSpec(memory_space=pl.ANY)
    layer_out, grad_inputs, grad_a, grad_b = pl.pallas_call(
        kernel,
        out_shape=(
            jax.ShapeDtypeStruct((1, T, W), BF16),
            jax.ShapeDtypeStruct((1, T, W), BF16),
            jax.ShapeDtypeStruct((3, R, W), F32),
            jax.ShapeDtypeStruct((3, R, W), F32),
        ),
        in_specs=[whole] * 3 + [anywhere] * 4,
        out_specs=(whole,) * 4,
        scratch_shapes=scratch,
        compiler_params=pltpu.CompilerParams(
            collective_id=0, has_side_effects=True, vmem_limit_bytes=48 * 1024 * 1024
        ),
        name="layer",
    )(inputs, output_gradient, adjacent, wqkv, wo, down, up)
    return layer_out, grad_inputs, jnp.swapaxes(grad_a, 1, 2), grad_b


def solution(mesh):
    return jax.shard_map(
        body,
        mesh=mesh,
        in_specs=(
            P("view", None, "head"),
            P("view", None, "head"),
            P(None, None, "head"),
            P("head", None),
            P(),
            P(None, None, "head"),
            P("view", None),
        ),
        out_specs=(
            P("view", None, "head"),
            P("view", None, "head"),
            P(None, "head", None),
            P(None, None, "head"),
        ),
        check_vma=False,
    )
```

profile of v0, /device:TPU:1, one launch (start us, length us, event | category | flops | bytes accessed | tf_op | source)
XLA Modules:
  0.0 107.6 jit_solution(18264429955272123144)
XLA Ops:
  0.6 1.0 copy.11.x_ref
  1.6 1.0 copy.12.og_ref
  2.6 2.3 %copy.14.down_hbm = bf16[3,1280,64]{2,1,0:T(8,128)(2,1)} copy(bf16[3,1280,64]{1,2,0:T(8,128)(2,1)} %param.11) | data formatting | bytes 983040 | tf_op args[4]
  5.0 0.0 copy-start.5
  5.0 4.0 %copy.13.wqkv_hbm = bf16[3,1280,320]{2,1,0:T(8,128)(2,1)S(1)} copy(bf16[3,1280,320]{1,2,0:T(8,128)(2,1)} %param.9) | data formatting | bytes 4915200 | tf_op args[2]
  9.0 0.0 copy-done.5
  9.0 0.0 copy-start
  9.1 1.2 %copy-done = bf16[3,1280,64]{2,1,0:T(8,128)(2,1)S(1)} copy-done((bf16[3,1280,64]{2,1,0:T(8,128)(2,1)S(1)}, bf16[3,1280,64]{2,1,0:T(8,128)(2,1)}, u32[]{:S(2)}) %copy-start) | copy-done | bytes 491544
  10.2 0.0 copy-start.1
  10.2 1.1 %copy-done.1 = bf16[320,1280]{1,0:T(8,128)(2,1)S(1)} copy-done((bf16[320,1280]{1,0:T(8,128)(2,1)S(1)}, bf16[320,1280]{1,0:T(8,128)(2,1)}, u32[]{:S(2)}) %copy-start.1) | copy-done | bytes 819224
  11.4 0.0 copy-start.3
  11.4 0.9 copy-done.3
  12.3 89.2 %layer.1 = (bf16[1,128,320]{2,1,0:T(8,128)(2,1)S(1)}, bf16[1,128,320]{2,1,0:T(8,128)(2,1)S(1)}, f32[3,64,320]{2,1,0:T(8,128)S(1)}, f32[3,64,320]{2,1,0:T(8,128)S(1)}) custom-call(bf16[1,128,320]{2,1,0:T(8,128)(2,1)S(1)} %copy.11.x_ref, bf16[1,128,320]{2,1,0:T(8,128)(2,1)S(1)} %copy.12.og_ref, s32[1,64]{1,0:T(1,128)S(1)} %copy-done.5, ...), custom_call_target="tpu_custom_call" | custom-call | tf_op jit(solution)/shard_map/layer/pallas_call | solution.py:564
  101.5 0.0 copy-start.2
  101.5 0.7 copy-done.2
  102.2 0.0 copy-start.4
  102.2 0.6 copy-done.4
  102.8 1.6 %copy.15 = bf16[1,128,320]{1,2,0:T(8,128)(2,1)} copy(bf16[1,128,320]{2,1,0:T(8,128)(2,1)} %copy-done.4) | data formatting | bytes 163840
  104.5 0.7 copy.16
  105.2 1.7 %copy.19 = f32[3,320,64]{1,2,0:T(8,128)} copy(f32[3,320,64]{1,2,0:T(8,128)} %bitcast.1) | data formatting | bytes 491520
  106.9 0.7 copy.20
Async XLA Ops:
  5.0 4.1 %copy-start.5 = (s32[1,64]{1,0:T(1,128)S(1)}, s32[1,64]{1,0:T(1,128)}, u32[]{:S(2)}) copy-start(s32[1,64]{1,0:T(1,128)} %adj_ref.1) | copy-start | bytes 772
  9.0 1.2 %copy-start = (bf16[3,1280,64]{2,1,0:T(8,128)(2,1)S(1)}, bf16[3,1280,64]{2,1,0:T(8,128)(2,1)}, u32[]{:S(2)}) copy-start(bf16[3,1280,64]{2,1,0:T(8,128)(2,1)} %copy.14.down_hbm) | copy-start | bytes 1474564
  10.2 1.1 %copy-start.1 = (bf16[320,1280]{1,0:T(8,128)(2,1)S(1)}, bf16[320,1280]{1,0:T(8,128)(2,1)}, u32[]{:S(2)}) copy-start(bf16[320,1280]{1,0:T(8,128)(2,1)} %wo_hbm.1) | copy-start | bytes 2457604
  11.4 0.9 copy-start.3
  101.5 0.7 copy-start.2
  102.2 0.6 copy-start.4
where the time goes:
time: 108 us
  Pallas kernels  89.2 us (83%)
  local copies, waits for them, and re-layouts  17.8 us (16%)
    pallas_call x1, Pallas kernels, body(): pl.pallas_call(kernel, out_shape=(jax.ShapeDtypeStruct((1, T, W), BF16),...  89.2 us
    unnamed x20, local copies, waits for them, and re-layouts  17.8 us

commit v1 on v0

v1 whole, which is shorter than its diff:
```python
import jax
import jax.numpy as jnp
from jax import lax
from jax.experimental import pallas as pl
from jax.experimental.pallas import tpu as pltpu
from jax.sharding import PartitionSpec as P

MESH = pl.DeviceIdType.MESH
F32 = jnp.float32
BF16 = jnp.bfloat16
T = 128
W = 320
D = 64
R = 64
ORDER = (0, 1, 2, 8, 5, 6, 7, 3, 4)
CHIPS = 32


def mm(a, b):
    return lax.dot_general(a, b, (((1,), (0,)), ((), ())), preferred_element_type=F32)


def mm_nt(a, b):
    return lax.dot_general(a, b, (((1,), (1,)), ((), ())), preferred_element_type=F32)


def kernel(
    adj_ref, x_hbm, og_hbm, wqkv_hbm, wo_hbm, down_hbm, up_hbm,
    lo_ref, gi_ref, ga_ref, gb_ref,
    wqkv, wo, down, up, wsem,
    xt, ogt, upt, downn, xsend, xrecv, ogsend, ogrecv,
    kv, qg, kvsend, kvrecv, kvbsend, kvbrecv, qgsend, qgrecv, qgbsend, qgbrecv,
    st, stsend, strecv,
    aq, ag, a4q, a4g, ak, av, a4kv, wtab,
    est, est4, oacc, o4acc, invb, delb, inv4, del4, dq, dq4, dk, dv, dkv4,
    att, gs, low, inacc, losrc, lobuf, losend, lorecv,
    gisrc, gibuf, gisend, girecv, lgall, *parts,
):
    view = lax.axis_index("view")
    head = lax.axis_index("head")
    chip = view // 2
    core = lax.rem(view, 2)
    z = view // 8
    y = lax.rem(chip, 4)
    spot = lax.rem(view, 8)
    sgn = 2 * core - 1

    def at(c, k):
        return (lax.rem(c + 2 * CHIPS, CHIPS) * 2 + k, head)

    def step(p, side):
        near = ((p + 1) // 2) * (2 * lax.rem(p, 2) - 1)
        if isinstance(p, int):
            return {7: 4 * side, 8: -4 * side}.get(p, near)
        return jnp.where(p == 7, 4 * side, jnp.where(p == 8, -4 * side, near))

    sibling = (chip * 2 + 1 - core, head)

    def z_peer(o):
        return (lax.rem(z + o, 8) * 8 + spot, head)

    def spot_peer(o):
        return (z * 8 + lax.rem(spot + o, 8), head)

    def x_peer(o):
        return (view, lax.rem(head + o, 4))

    def remote(src, dst, ss, rs, dev):
        return pltpu.make_async_remote_copy(
            src_ref=src, dst_ref=dst, send_sem=ss, recv_sem=rs,
            device_id=dev, device_id_type=MESH,
        )

    mine = pl.ds(pl.multiple_of(head * W, 64), W)
    loads = [
        pltpu.make_async_copy(s, d, wsem.at[i])
        for i, (s, d) in enumerate(
            (
                (x_hbm.at[0], xt.at[mine]), (down_hbm, down), (up_hbm, up), (wqkv_hbm, wqkv),
                (og_hbm.at[0], ogt.at[mine]), (wo_hbm, wo),
            )
        )
    ]
    for load in loads:
        load.start()

    barrier = pltpu.get_barrier_semaphore()

    def greet(dev):
        pl.semaphore_signal(barrier, inc=1, device_id=dev, device_id_type=MESH)

    for o in (1, 2, 3):
        greet(x_peer(o))

    @pl.loop(1, 9)
    def _(o):
        greet((lax.rem(view + o, 64), head))
        greet((lax.rem(view + 64 - o, 64), head))

    for o in (2, 3, 4, 5, 6):
        greet(z_peer(o))
    pl.semaphore_wait(barrier, 24)

    def x_copy(o):
        return remote(x_hbm.at[0], xt.at[mine], xsend.at[o], xrecv.at[o], x_peer(o))

    def og_copy(o):
        return remote(og_hbm.at[0], ogt.at[mine], ogsend.at[o], ogrecv.at[o], x_peer(o))

    for o in (1, 3, 2):
        x_copy(o).start()

    adj = adj_ref[...].astype(F32)
    lane64 = lax.broadcasted_iota(jnp.int32, (1, 64), 1)

    def weight_of(v):
        one = jnp.sum(jnp.where(lane64 == v, adj, 0.0), axis=1, keepdims=True)
        return jnp.broadcast_to(one, (1, T))

    for p in range(9):
        c = lax.rem(chip + step(p, sgn) + 2 * CHIPS, CHIPS) * 2
        wtab[p : p + 1, 0:T] = weight_of(c + core)
        wtab[p : p + 1, T : 2 * T] = weight_of(c + 1 - core)
    lane = lax.broadcasted_iota(jnp.int32, (T, T), 1)
    left = lane < D

    def block_diagonal(dst, i, tile):
        zero = jnp.zeros_like(tile)
        dst[i, 0:T, :] = jnp.where(left, tile, zero)
        dst[i, T : 2 * T, :] = jnp.where(left, zero, tile)

    for load in loads[1:3]:
        load.wait()
    for m in range(3):
        upt[m] = jnp.transpose(up[R * m : R * (m + 1), :])
    for h in range(10):
        downn[T * h : T * (h + 1), :] = jnp.transpose(down[:, T * h : T * (h + 1)])

    loads[3].wait()
    loads[0].wait()
    for o in (1, 2, 3):
        x_copy(o).wait_recv()
    for o in (1, 3, 2):
        og_copy(o).start()
    low[...] = mm(down[...], xt[...]).astype(BF16)

    def project(m):
        main = mm(wqkv[W * m : W * (m + 1), :], xt[...])
        return (main + 0.5 * mm(upt[m], low[R * m : R * (m + 1), :])).astype(BF16)

    def lay_out(buf, first, second):
        for i in range(2):
            part = slice(T * i, T * (i + 1))
            buf[0:T, T * i : T * (i + 1)] = jnp.transpose(first[part])
            buf[0:T, 256 + T * i : 256 + T * (i + 1)] = jnp.transpose(second[part])
        both = jnp.concatenate([first[256:320], second[256:320]], axis=0)
        buf[0:T, 512:640] = jnp.transpose(both)

    lay_out(kv, project(1), project(2))

    def pair_rows(p):
        return pl.ds(pl.multiple_of(p * 256, 256), T)

    def sib_rows(p):
        return pl.ds(pl.multiple_of(p * 256 + T, T), T)

    def sib_copy(buf, ss, rs, p, into):
        return remote(
            buf.at[pair_rows(p)], buf.at[sib_rows(into)], ss.at[into], rs.at[into], sibling
        )

    class Blocks:
        def __init__(self, buf, ss, rs, bs, br):
            self.buf, self.ss, self.rs, self.bs, self.br = buf, ss, rs, bs, br

        def copy(self, p):
            return remote(
                self.buf.at[0:T], self.buf.at[pair_rows(p)], self.ss.at[p], self.rs.at[p],
                at(chip - step(p, sgn), core),
            )

        def start_own(self):
            self.sib(0).start()
            for p in ORDER[1:]:
                self.copy(p).start()

        def sib(self, p):
            return sib_copy(self.buf, self.bs, self.br, p, 7 if p == 8 else p)

        def arrive(self, *ps):
            for p in ps:
                self.copy(p).wait_recv()
                if p != 7:
                    self.sib(p).start()

        def sib_arrived(self, p):
            if p != 8:
                self.sib(8 if p == 7 else p).wait_recv()

        def drain(self):
            for p in range(9):
                if p > 0:
                    self.copy(p).wait_send()
                if p != 7:
                    self.sib(p).wait_send()

    keys = Blocks(kv, kvsend, kvrecv, kvbsend, kvbrecv)
    queries = Blocks(qg, qgsend, qgrecv, qgbsend, qgbrecv)
    keys.start_own()
    query = project(0)
    loads[5].wait()
    loads[4].wait()
    for o in (1, 2, 3):
        og_copy(o).wait_recv()
    lay_out(qg, query, mm(wo[...], ogt[...]).astype(BF16))
    queries.start_own()

    eighth = jnp.asarray(0.125, BF16)
    for i in range(2):
        block_diagonal(aq, i, qg[0:T, T * i : T * (i + 1)] * eighth)
        block_diagonal(ag, i, qg[0:T, 256 + T * i : 256 + T * (i + 1)])
        block_diagonal(ak, i, kv[0:T, T * i : T * (i + 1)] * eighth)
        block_diagonal(av, i, kv[0:T, 256 + T * i : 256 + T * (i + 1)])
    tile = qg[0:T, 512:640]
    a4q[...] = jnp.where(left, tile * eighth, jnp.zeros_like(tile))
    a4g[...] = jnp.where(left, jnp.zeros_like(tile), tile)
    tile = kv[0:T, 512:640]
    a4kv[0:T, :] = jnp.where(left, tile * eighth, jnp.zeros_like(tile))
    a4kv[T : 2 * T, :] = jnp.where(left, jnp.zeros_like(tile), tile)

    oacc[...] = jnp.zeros_like(oacc)
    o4acc[...] = jnp.zeros_like(o4acc)
    dq[...] = jnp.zeros_like(dq)
    dq4[...] = jnp.zeros_like(dq4)
    dk[...] = jnp.zeros_like(dk)
    dv[...] = jnp.zeros_like(dv)
    dkv4[...] = jnp.zeros_like(dkv4)

    def block(buf, p, n):
        span = pl.ds(pl.multiple_of(p * 256, 256), n)
        return [buf[span, T * i : T * (i + 1)] for i in range(5)]

    def forward(p, n):
        k0, k1, v0, v1, kv4 = block(kv, p, n)
        weight = wtab[pl.ds(p, 1), 0:n]
        ones = jnp.ones((n, T), BF16)
        for i, (k, v) in enumerate(((k0, v0), (k1, v1))):
            e = (jnp.exp(mm_nt(aq[i], k)) * weight).astype(BF16)
            est[p, i, :, 0:n] = e
            oacc[i] += mm(e, jnp.concatenate([v, ones], axis=1))
        e = (jnp.exp(mm_nt(a4q[...], kv4)) * weight).astype(BF16)
        est4[p, :, 0:n] = e
        o4acc[...] += mm(e, jnp.concatenate([kv4, ones], axis=1))

    def run(work, blocks, order):
        for p in order:
            if blocks is not None:
                blocks.sib_arrived(p)
            work(p, T if p == 8 else 256)

    previous = 0
    for p in ORDER[1:]:
        keys.arrive(p)
        run(forward, keys, (previous,))
        previous = p
    run(forward, keys, (previous,))

    def diagonal(a):
        return jnp.where(left, a[0:T], a[T : 2 * T])

    stats = jnp.zeros((T, T), F32)

    def put(stats, i, column):
        return jnp.where(lane == i, column, stats)

    for i in range(2):
        inv = 1.0 / oacc[i, :, T : 2 * T]
        invb[i] = inv
        pair = diagonal(oacc[i, :, 0:T] * inv).astype(BF16)
        att[:, T * i : T * (i + 1)] = pair
        prod = pair.astype(F32) * qg[0:T, 256 + T * i : 256 + T * (i + 1)].astype(F32)
        first = jnp.sum(jnp.where(left, prod, 0.0), axis=1, keepdims=True)
        second = jnp.sum(jnp.where(left, 0.0, prod), axis=1, keepdims=True)
        delb[i, 0:T, :] = jnp.broadcast_to(first, (T, T))
        delb[i, T : 2 * T, :] = jnp.broadcast_to(second, (T, T))
        stats = put(stats, 2 * i, inv[0:T])
        stats = put(stats, 2 * i + 1, inv[T : 2 * T])
        stats = put(stats, 5 + 2 * i, first)
        stats = put(stats, 6 + 2 * i, second)
    inv = 1.0 / o4acc[:, T : 2 * T]
    inv4[...] = inv
    last = (o4acc[:, 0:T] * inv).astype(BF16)
    att[:, 256:320] = last[:, D:T]
    prod = last.astype(F32) * qg[0:T, 512:640].astype(F32)
    first = jnp.sum(jnp.where(left, 0.0, prod), axis=1, keepdims=True)
    del4[...] = jnp.broadcast_to(first, (T, T))
    stats = put(stats, 4, inv)
    stats = put(stats, 9, first)
    st[0, 0] = jnp.transpose(stats)[0:16, :]
    st[0, 0, 10:11, 0:64] = adj

    def stb_copy():
        return remote(st.at[0, 0], st.at[0, 1], stsend.at[0], strecv.at[0], sibling)

    def st_copy(p):
        return remote(
            st.at[0], st.at[p], stsend.at[p], strecv.at[p], at(chip - step(p, sgn), core)
        )

    stb_copy().start()
    stb_copy().wait_recv()
    for p in ORDER[1:]:
        st_copy(p).start()

    share = mm(att[...], wo[...]).astype(BF16)
    for h in range(4):
        losrc[h] = share[:, W * h : W * (h + 1)]

    def lo_copy(o):
        return remote(
            losrc.at[lax.rem(head + o, 4)], lobuf.at[o], losend.at[o], lorecv.at[o], x_peer(o)
        )

    for o in (1, 2, 3):
        lo_copy(o).start()

    def wide(a, n):
        return a if n == T else jnp.concatenate([a, a], axis=1)

    def backward_q(p, n):
        k0, k1, v0, v1, kv4 = block(kv, p, n)
        for i, (k, v) in enumerate(((k0, v0), (k1, v1))):
            prob = est[p, i, :, 0:n].astype(F32) * wide(invb[i], n)
            dl = prob * (mm_nt(ag[i], v) - wide(delb[i], n))
            dq[i] += mm(dl.astype(BF16), k)
        prob = est4[p, :, 0:n].astype(F32) * wide(inv4[...], n)
        dl = prob * (mm_nt(a4g[...], kv4) - wide(del4[...], n))
        dq4[...] += mm(dl.astype(BF16), kv4)

    run(backward_q, None, ORDER)
    for i in range(2):
        gs[0, :, T * i : T * (i + 1)] = (diagonal(dq[i]) * 0.125).astype(BF16)
    gs[0, :, 256:320] = (dq4[:, 0:D] * 0.125).astype(BF16)

    class Adapters:
        def __init__(self, which, lgsrc, lgbuf, acc, accb, rsbuf, zbuf, fin, sems):
            self.which, self.lgsrc, self.lgbuf = which, lgsrc, lgbuf
            self.acc, self.accb, self.rsbuf, self.zbuf, self.fin = acc, accb, rsbuf, zbuf, fin
            self.sems = sems
            self.count = R * len(which)
            self.share = self.count // 4

        def part(self, i):
            return pl.ds(pl.multiple_of(i * self.share, 16), self.share)

        def copies(self, stage):
            def copy(o):
                ends = {
                    0: lambda: (self.lgsrc, self.lgbuf.at[o], x_peer(o)),
                    1: lambda: (
                        self.accb.at[self.part(lax.rem(spot + o, 8))], self.rsbuf.at[o], spot_peer(o)
                    ),
                    2: lambda: (self.zbuf.at[z], self.zbuf.at[z], z_peer(o)),
                    3: lambda: (self.fin.at[spot], self.fin.at[spot], spot_peer(o)),
                }
                src, dst, dev = ends[stage]()
                return remote(src, dst, self.sems.at[stage, 0, o], self.sems.at[stage, 1, o], dev)

            return [copy(o) for o in range(1, 8 if stage else 4)]

        def start(self, stage):
            for c in self.copies(stage):
                c.start()

        def wait(self, stage):
            for c in self.copies(stage):
                c.wait_recv()

        def send_low(self):
            for i, m in enumerate(self.which):
                one = 0.5 * mm_nt(up[R * m : R * (m + 1), :], gs[m])
                self.lgsrc[R * i : R * (i + 1), :] = one.astype(BF16)
            self.start(0)
            for i, m in enumerate(self.which):
                self.acc[self.count + R * i : self.count + R * (i + 1), :] = 0.5 * mm(
                    low[R * m : R * (m + 1), :], gs[m]
                )

        def send_plane(self):
            self.wait(0)
            lg = self.lgsrc[...].astype(F32)
            for o in (1, 2, 3):
                lg = lg + self.lgbuf[o].astype(F32)
            lg = lg.astype(BF16)
            lgall[R * self.which[0] : R * self.which[0] + self.count, :] = lg
            self.acc[0 : self.count, :] = mm_nt(lg, xt[mine, :])
            self.accb[...] = self.acc[...].astype(BF16)
            self.start(1)

        def send_z(self):
            self.wait(1)
            total = self.acc[self.part(spot), :]
            for o in range(1, 8):
                total = total + self.rsbuf[o].astype(F32)
            self.zbuf[z] = total.astype(BF16)
            self.start(2)

        def send_back(self):
            self.wait(2)
            total = self.zbuf[0].astype(F32)
            for i in range(1, 8):
                total = total + self.zbuf[i].astype(F32)
            self.fin[spot] = total.astype(BF16)
            self.start(3)

        def finish(self):
            self.wait(3)
            for i in range(8):
                for r in range(0, self.share, 16):
                    which, at_row = divmod((i % 4) * self.share + r, R)
                    out = ga_ref if i < 4 else gb_ref
                    rows = slice(at_row, at_row + 16)
                    out[self.which[which], rows, :] = self.fin[i, r : r + 16, :].astype(F32)

        def drain(self):
            for stage in range(4):
                for c in self.copies(stage):
                    c.wait_send()

    late = Adapters((0, 1, 2), *parts)
    inacc[...] = mm(gs[0], wqkv[0:W, :])

    me_lane = lax.broadcasted_iota(jnp.int32, (1, T), 1) == view

    def backward_kv(p, n):
        q0, q1, g0, g1, qg4 = block(qg, p, n)
        sides = [st[p, s] for s in range(n // T)]
        invs, deltas = [], []
        for s in sides:
            w = jnp.sum(jnp.where(me_lane, s[10:11, :], 0.0), axis=1, keepdims=True)
            invs.append(s * w)
        invs = invs[0] if n == T else jnp.concatenate(invs, axis=1)
        deltas = sides[0] if n == T else jnp.concatenate(sides, axis=1)

        def weigh(e, h):
            return e * invs[h : h + 1, :]

        def shift(dp, h):
            return dp - deltas[5 + h : 6 + h, :]

        for i, (q, g) in enumerate(((q0, g0), (q1, g1))):
            e = jnp.exp(mm_nt(ak[i], q))
            dp = mm_nt(av[i], g)
            prob = [weigh(e[0:T], 2 * i), weigh(e[T : 2 * T], 2 * i + 1)]
            dl = [prob[0] * shift(dp[0:T], 2 * i), prob[1] * shift(dp[T : 2 * T], 2 * i + 1)]
            prob = jnp.concatenate(prob, axis=0).astype(BF16)
            dl = jnp.concatenate(dl, axis=0).astype(BF16)
            dk[i] += mm(dl, q)
            dv[i] += mm(prob, g)
        both = mm_nt(a4kv[...], qg4)
        prob = weigh(jnp.exp(both[0:T]), 4)
        dl = prob * shift(both[T : 2 * T], 4)
        dkv4[...] += mm(jnp.concatenate([dl, prob], axis=0).astype(BF16), qg4)

    def run_kv(*order):
        for p in order:
            if p != 0:
                st_copy(p).wait_recv()
        run(backward_kv, queries, order)

    queries.arrive(1, 2, 8, 5, 6, 7, 3, 4)
    run_kv(*ORDER)
    for i in range(2):
        gs[1, :, T * i : T * (i + 1)] = (diagonal(dk[i]) * 0.125).astype(BF16)
        gs[2, :, T * i : T * (i + 1)] = diagonal(dv[i]).astype(BF16)
    gs[1, :, 256:320] = (dkv4[0:T, 0:D] * 0.125).astype(BF16)
    gs[2, :, 256:320] = dkv4[T : 2 * T, D:T].astype(BF16)

    late.send_low()

    share = inacc[...] + mm(gs[1], wqkv[W : 2 * W, :]) + mm(gs[2], wqkv[2 * W : 3 * W, :])
    share = share.astype(BF16)
    for h in range(4):
        gisrc[h] = share[:, W * h : W * (h + 1)]

    def gi_copy(o):
        return remote(
            gisrc.at[lax.rem(head + o, 4)], gibuf.at[o], gisend.at[o], girecv.at[o], x_peer(o)
        )

    for o in (1, 2, 3):
        gi_copy(o).start()
    late.send_plane()

    own = gisrc[head].astype(F32)
    for o in (1, 2, 3):
        gi_copy(o).wait_recv()
        own = own + gibuf[o].astype(F32)
    gi_ref[0] = (jnp.transpose(own) + mm(downn[mine, :], lgall[...])).astype(BF16)
    out = losrc[head].astype(F32)
    for o in (1, 2, 3):
        lo_copy(o).wait_recv()
        out = out + lobuf[o].astype(F32)
    lo_ref[0] = jnp.transpose(out).astype(BF16)

    late.send_z()
    late.send_back()
    late.finish()

    for o in (1, 2, 3):
        x_copy(o).wait_send()
        og_copy(o).wait_send()
        lo_copy(o).wait_send()
        gi_copy(o).wait_send()
    keys.drain()
    queries.drain()

    stb_copy().wait_send()
    for p in ORDER[1:]:
        st_copy(p).wait_send()
    late.drain()


def hand_over(*refs):
    source, target, held, sem = refs[0:4], refs[4:8], refs[8:12], refs[12]
    into = [pltpu.make_async_copy(s, h, sem.at[0, i]) for i, (s, h) in enumerate(zip(source, held))]
    out = [pltpu.make_async_copy(h, t, sem.at[1, i]) for i, (h, t) in enumerate(zip(held, target))]
    for copy in into:
        copy.start()
    for first, second in zip(into, out):
        first.wait()
        second.start()
    for copy in out:
        copy.wait()


def body(inputs, output_gradient, wqkv, wo, down, up, adjacent):
    vmem = pltpu.VMEM
    dma = pltpu.SemaphoreType.DMA
    scratch = [
        vmem((3 * W, 1280), BF16), vmem((W, 1280), BF16), vmem((3 * R, 1280), BF16),
        vmem((3 * R, W), BF16), dma((6,)),
        vmem((1280, T), BF16), vmem((1280, T), BF16), vmem((3, W, R), BF16),
        vmem((1280, 3 * R), BF16), dma((4,)), dma((4,)), dma((4,)), dma((4,)),
        vmem((17 * T, 640), BF16), vmem((17 * T, 640), BF16),
        dma((9,)), dma((9,)), dma((8,)), dma((8,)), dma((9,)), dma((9,)), dma((8,)), dma((8,)),
        vmem((9, 2, 16, T), F32), dma((9,)), dma((9,)),
        vmem((2, 256, T), BF16), vmem((2, 256, T), BF16), vmem((T, T), BF16), vmem((T, T), BF16),
        vmem((2, 256, T), BF16), vmem((2, 256, T), BF16), vmem((256, T), BF16),
        vmem((16, 256), F32),
        vmem((9, 2, 256, 256), BF16), vmem((9, T, 256), BF16), vmem((2, 256, 256), F32),
        vmem((T, 256), F32), vmem((2, 256, T), F32), vmem((2, 256, T), F32), vmem((T, T), F32),
        vmem((T, T), F32), vmem((2, 256, T), F32), vmem((T, T), F32), vmem((2, 256, T), F32),
        vmem((2, 256, T), F32), vmem((256, T), F32),
        vmem((T, W), BF16), vmem((3, T, W), BF16), vmem((3 * R, T), BF16), vmem((T, 1280), F32),
        vmem((4, T, W), BF16), vmem((4, T, W), BF16), dma((4,)), dma((4,)),
        vmem((4, T, W), BF16), vmem((4, T, W), BF16), dma((4,)), dma((4,)), vmem((3 * R, T), BF16),
    ]
    share = vmem((8, 6 * R // 8, W), BF16)
    scratch += [vmem((3 * R, T), BF16), vmem((4, 3 * R, T), BF16), vmem((6 * R, W), F32)]
    scratch += [vmem((6 * R, W), BF16), share, share, share, dma((4, 2, 8))]
    whole = pl.BlockSpec(memory_space=pltpu.VMEM)
    hbm = pl.BlockSpec(memory_space=pltpu.HBM)
    results = pl.pallas_call(
        kernel,
        out_shape=(
            jax.ShapeDtypeStruct((1, W, T), BF16),
            jax.ShapeDtypeStruct((1, W, T), BF16),
            jax.ShapeDtypeStruct((3, R, W), F32),
            jax.ShapeDtypeStruct((3, R, W), F32),
        ),
        in_specs=[whole] + [hbm] * 6,
        out_specs=(whole,) * 4,
        scratch_shapes=scratch,
        compiler_params=pltpu.CompilerParams(
            collective_id=0, has_side_effects=True, vmem_limit_bytes=62 * 1024 * 1024
        ),
        name="layer",
    )(
        adjacent,
        jnp.swapaxes(inputs, 1, 2),
        jnp.swapaxes(output_gradient, 1, 2),
        jnp.swapaxes(wqkv, 1, 2).reshape(3 * W, 1280),
        wo,
        jnp.swapaxes(down, 1, 2).reshape(3 * R, 1280),
        up.reshape(3 * R, W),
    )
    layer_out, grad_inputs, grad_a, grad_b = pl.pallas_call(
        hand_over,
        out_shape=tuple(jax.ShapeDtypeStruct(r.shape, r.dtype) for r in results),
        in_specs=[hbm] * 4,
        out_specs=(hbm,) * 4,
        scratch_shapes=[vmem(r.shape, r.dtype) for r in results] + [dma((2, 4))],
        compiler_params=pltpu.CompilerParams(vmem_limit_bytes=62 * 1024 * 1024),
        name="hand_over",
    )(*results)
    return (
        jnp.swapaxes(layer_out, 1, 2),
        jnp.swapaxes(grad_inputs, 1, 2),
        jnp.swapaxes(grad_a, 1, 2),
        grad_b,
    )


def solution(mesh):
    return jax.shard_map(
        body,
        mesh=mesh,
        in_specs=(
            P("view", None, "head"),
            P("view", None, "head"),
            P(None, None, "head"),
            P("head", None),
            P(),
            P(None, None, "head"),
            P("view", None),
        ),
        out_specs=(
            P("view", None, "head"),
            P("view", None, "head"),
            P(None, "head", None),
            P(None, None, "head"),
        ),
        check_vma=False,
    )
```

time: 108 us -> 89.5 us (0.83)
  local copies, waits for them, and re-layouts: 17.8 us -> 0 us
    unnamed x20 -> x0, local copies, waits for them, and re-layouts: 17.8 us -> none
    pallas_call x1 -> x2, Pallas kernels: 89.2 us -> 88.8 us  [the longest x1 86.9 us: body(): pl.pallas_call(kernel, out_shape=(jax.ShapeDtypeStruct((1, W, T), BF16),...]
where the time goes in v1:
time: 89.5 us; the launch traced here: 89.4 us
  Pallas kernels  88.8 us (99%)
    pallas_call x1, Pallas kernels, body(): pl.pallas_call(kernel, out_shape=(jax.ShapeDtypeStruct((1, W, T), BF16),...  86.9 us
    pallas_call x1, Pallas kernels, body(): pl.pallas_call(hand_over, out_shape=tuple((jax.ShapeDtypeStruct(r.shape,...  1.93 us

profile of v1, /device:TPU:1, one launch (start us, length us, event | category | flops | bytes accessed | tf_op | source)
XLA Modules:
  0.0 89.4 jit_solution(10932507908921127387)
XLA Ops:
  0.6 86.9 %layer.1 = (bf16[1,320,128]{2,1,0:T(8,128)(2,1)}, bf16[1,320,128]{2,1,0:T(8,128)(2,1)}, f32[3,64,320]{2,1,0:T(8,128)}, f32[3,64,320]{2,1,0:T(8,128)}) custom-call(s32[1,64]{1,0:T(1,128)} %adj_ref.1, bf16[1,320,128]{2,1,0:T(8,128)(2,1)} %bitcast.15, bf16[1,320,128]{2,1,0:T(8,128)(2,1)} %bitcast.16, bf16[960,1280]{1,0:T(8,128)(2,1)} %bitcast.12, ...), custom_call_target="tpu_custom_call" | custom-call | tf_op jit(solution)/shard_map/layer/pallas_call | solution.py:564
  87.5 1.9 %hand_over.1 = (bf16[1,320,128]{2,1,0:T(8,128)(2,1)}, bf16[1,320,128]{2,1,0:T(8,128)(2,1)}, f32[3,64,320]{2,1,0:T(8,128)}, f32[3,64,320]{2,1,0:T(8,128)}) custom-call(bf16[1,320,128]{2,1,0:T(8,128)(2,1)} %get-tuple-element.12.refs_0_, bf16[1,320,128]{2,1,0:T(8,128)(2,1)} %get-tuple-element.13.refs_1_, f32[3,64,320]{2,1,0:T(8,128)} %get-tuple-element.14.refs_2_, ...), custom_call_target="tpu_custom_call" | custom-call | tf_op jit(solution)/shard_map/hand_over/pallas_call | solution.py:588

commit v2 on v1

--- a/solution.py
+++ b/solution.py
@@ -29,10 +29,11 @@
     lo_ref, gi_ref, ga_ref, gb_ref,
     wqkv, wo, down, up, wsem,
     xt, ogt, upt, downn, xsend, xrecv, ogsend, ogrecv,
+    kvo, qgo, kvm, qgm, kvmsems, qgmsems, adjq, adjsems, stm, stmsems, ret, retbuf, retsems,
+    aqm, agm, akm, avm, wq, wk, estm, om, invm, delm, dqm, dkm, dvm,
     kv, qg, kvsend, kvrecv, kvbsend, kvbrecv, qgsend, qgrecv, qgbsend, qgbrecv,
     st, stsend, strecv,
-    aq, ag, a4q, a4g, ak, av, a4kv, wtab,
-    est, est4, oacc, o4acc, invb, delb, inv4, del4, dq, dq4, dk, dv, dkv4,
+    a4q, a4g, a4kv, wtab, est4, o4acc, inv4, del4, dq4, dkv4,
     att, gs, low, inacc, losrc, lobuf, losend, lorecv,
     gisrc, gibuf, gisend, girecv, lgall, *parts,
 ):
@@ -124,10 +125,17 @@
     lane = lax.broadcasted_iota(jnp.int32, (T, T), 1)
     left = lane < D
 
-    def block_diagonal(dst, i, tile):
-        zero = jnp.zeros_like(tile)
-        dst[i, 0:T, :] = jnp.where(left, tile, zero)
-        dst[i, T : 2 * T, :] = jnp.where(left, zero, tile)
+    def column(o):
+        return (z * 8 + lax.rem(y + o, 4) * 2 + core, head)
+
+    row = jnp.concatenate([adj, jnp.zeros((1, 64), F32)], axis=1)
+    adjq[y] = jnp.broadcast_to(row, (8, T))
+
+    def adj_copy(o):
+        return remote(adjq.at[y], adjq.at[y], adjsems.at[0, o], adjsems.at[1, o], column(o))
+
+    for o in (1, 3, 2):
+        adj_copy(o).start()
 
     for load in loads[1:3]:
         load.wait()
@@ -148,15 +156,16 @@
         main = mm(wqkv[W * m : W * (m + 1), :], xt[...])
         return (main + 0.5 * mm(upt[m], low[R * m : R * (m + 1), :])).astype(BF16)
 
-    def lay_out(buf, first, second):
-        for i in range(2):
-            part = slice(T * i, T * (i + 1))
-            buf[0:T, T * i : T * (i + 1)] = jnp.transpose(first[part])
-            buf[0:T, 256 + T * i : 256 + T * (i + 1)] = jnp.transpose(second[part])
-        both = jnp.concatenate([first[256:320], second[256:320]], axis=0)
-        buf[0:T, 512:640] = jnp.transpose(both)
-
-    lay_out(kv, project(1), project(2))
+    def lay_out(out, buf, first, second):
+        for h in range(5):
+            part = slice(D * h, D * (h + 1))
+            tile = jnp.transpose(jnp.concatenate([first[part], second[part]], axis=0))
+            if h < 4:
+                out[h] = tile
+            else:
+                buf[0:T, :] = tile
+
+    lay_out(kvo, kv, project(1), project(2))
 
     def pair_rows(p):
         return pl.ds(pl.multiple_of(p * 256, 256), T)
@@ -204,53 +213,129 @@
                 if p != 7:
                     self.sib(p).wait_send()
 
+    def span(group):
+        return slice(512 * group, 512 * (group + 1))
+
+    class Planes:
+        def __init__(self, out, buf, sems):
+            self.out, self.buf, self.sems = out, buf, sems
+
+        def swap(self, o):
+            return remote(
+                self.out.at[lax.rem(y + o, 4)], self.buf.at[pl.ds(pl.multiple_of(y * T, T), T)],
+                self.sems.at[0, o], self.sems.at[1, o], column(o),
+            )
+
+        def group(self, src, into, dev):
+            return remote(
+                self.buf.at[span(src)], self.buf.at[span(into)],
+                self.sems.at[0, 4 + into], self.sems.at[1, 4 + into], dev,
+            )
+
+        def move(self, into):
+            if into in (2, 4):
+                return self.group(0, into, z_peer(1 if into == 2 else 7))
+            return self.group(into - 1, into, sibling)
+
+        def start(self):
+            for o in (1, 3, 2):
+                self.swap(o).start()
+            self.buf[pl.ds(pl.multiple_of(y * T, T), T), :] = self.out[y]
+
+        def swapped(self):
+            for o in (1, 3, 2):
+                self.swap(o).wait_recv()
+            for g in (2, 4, 1):
+                self.move(g).start()
+
+        def arrive(self, group):
+            self.move(group).wait_recv()
+            if group in (2, 4):
+                self.move(group + 1).start()
+
+        def drain(self):
+            for o in (1, 2, 3):
+                self.swap(o).wait_send()
+            for g in range(1, 6):
+                self.move(g).wait_send()
+
+    plane_keys = Planes(kvo, kvm, kvmsems)
+    plane_queries = Planes(qgo, qgm, qgmsems)
     keys = Blocks(kv, kvsend, kvrecv, kvbsend, kvbrecv)
     queries = Blocks(qg, qgsend, qgrecv, qgbsend, qgbrecv)
+    plane_keys.start()
+    query = project(0)
+    plane_keys.swapped()
     keys.start_own()
-    query = project(0)
     loads[5].wait()
     loads[4].wait()
     for o in (1, 2, 3):
         og_copy(o).wait_recv()
-    lay_out(qg, query, mm(wo[...], ogt[...]).astype(BF16))
+    lay_out(qgo, qg, query, mm(wo[...], ogt[...]).astype(BF16))
+    plane_queries.start()
+
+    for o in (1, 2, 3):
+        adj_copy(o).wait_recv()
+    rows4 = jnp.concatenate([adjq[i, 0:1, :] for i in range(4)], axis=0)
+    lane4 = lax.broadcasted_iota(jnp.int32, (4, T), 1)
+    sub4 = lax.broadcasted_iota(jnp.int32, (4, T), 0)
+
+    def view_of(group, i):
+        plane = lax.rem(z + (0, 7, 1)[group // 2], 8)
+        return plane * 8 + 2 * i + (core if group % 2 == 0 else 1 - core)
+
+    for g in range(6):
+        for i in range(4):
+            one = jnp.sum(jnp.where(lane4 == view_of(g, i), rows4, 0.0), axis=1, keepdims=True)
+            wq[2 * g + i // 2, 0:4, T * (i % 2) : T * (i % 2 + 1)] = jnp.broadcast_to(one, (4, T))
+
+    plane_queries.swapped()
     queries.start_own()
 
+    def tall(a, n):
+        return jnp.concatenate([a] * n, axis=0)
+
     eighth = jnp.asarray(0.125, BF16)
-    for i in range(2):
-        block_diagonal(aq, i, qg[0:T, T * i : T * (i + 1)] * eighth)
-        block_diagonal(ag, i, qg[0:T, 256 + T * i : 256 + T * (i + 1)])
-        block_diagonal(ak, i, kv[0:T, T * i : T * (i + 1)] * eighth)
-        block_diagonal(av, i, kv[0:T, 256 + T * i : 256 + T * (i + 1)])
-    tile = qg[0:T, 512:640]
+    tile = qg[0:T, :]
     a4q[...] = jnp.where(left, tile * eighth, jnp.zeros_like(tile))
     a4g[...] = jnp.where(left, jnp.zeros_like(tile), tile)
-    tile = kv[0:T, 512:640]
+    tile = kv[0:T, :]
     a4kv[0:T, :] = jnp.where(left, tile * eighth, jnp.zeros_like(tile))
     a4kv[T : 2 * T, :] = jnp.where(left, jnp.zeros_like(tile), tile)
-
-    oacc[...] = jnp.zeros_like(oacc)
-    o4acc[...] = jnp.zeros_like(o4acc)
-    dq[...] = jnp.zeros_like(dq)
-    dq4[...] = jnp.zeros_like(dq4)
-    dk[...] = jnp.zeros_like(dk)
-    dv[...] = jnp.zeros_like(dv)
-    dkv4[...] = jnp.zeros_like(dkv4)
+    for i in range(4):
+        part = slice(T * i, T * (i + 1))
+        tile = qgm[part, :]
+        aqm[part, :] = jnp.where(left, tile * eighth, jnp.zeros_like(tile))
+        agm[part, :] = jnp.where(left, jnp.zeros_like(tile), tile)
+        tile = kvm[part, :]
+        akm[part, :] = jnp.where(left, tile * eighth, jnp.zeros_like(tile))
+        avm[part, :] = jnp.where(left, jnp.zeros_like(tile), tile)
+
+    for ref in (om, dqm, dkm, dvm, o4acc, dq4, dkv4):
+        ref[...] = jnp.zeros_like(ref)
 
     def block(buf, p, n):
-        span = pl.ds(pl.multiple_of(p * 256, 256), n)
-        return [buf[span, T * i : T * (i + 1)] for i in range(5)]
+        return buf[pl.ds(pl.multiple_of(p * 256, 256), n), :]
 
     def forward(p, n):
-        k0, k1, v0, v1, kv4 = block(kv, p, n)
+        kv4 = block(kv, p, n)
         weight = wtab[pl.ds(p, 1), 0:n]
         ones = jnp.ones((n, T), BF16)
-        for i, (k, v) in enumerate(((k0, v0), (k1, v1))):
-            e = (jnp.exp(mm_nt(aq[i], k)) * weight).astype(BF16)
-            est[p, i, :, 0:n] = e
-            oacc[i] += mm(e, jnp.concatenate([v, ones], axis=1))
-        e = (jnp.exp(mm_nt(a4q[...], kv4)) * weight).astype(BF16)
+        e = jnp.where(weight > 0.0, jnp.exp(mm_nt(a4q[...], kv4)), 0.0).astype(BF16)
         est4[p, :, 0:n] = e
         o4acc[...] += mm(e, jnp.concatenate([kv4, ones], axis=1))
+
+    def masked(weights, e):
+        parts = [
+            jnp.where(weights[i : i + 1, :] > 0.0, e[T * i : T * (i + 1)], 0.0) for i in range(4)
+        ]
+        return jnp.concatenate(parts, axis=0)
+
+    def forward_plane(t):
+        tile = block(kvm, t, 256)
+        e = masked(wq[t], jnp.exp(mm_nt(aqm[...], tile))).astype(BF16)
+        estm[t] = e
+        om[...] += mm(e, jnp.concatenate([tile, jnp.ones((256, T), BF16)], axis=1))
 
     def run(work, blocks, order):
         for p in order:
@@ -258,46 +343,58 @@
                 blocks.sib_arrived(p)
             work(p, T if p == 8 else 256)
 
-    previous = 0
+    def run_plane(work, *groups):
+        for g in groups:
+            pl.loop(2 * g, 2 * g + 2)(work)
+
+    run_plane(forward_plane, 0)
+    plane_keys.arrive(2)
+    plane_keys.arrive(4)
+    plane_keys.arrive(1)
+    run_plane(forward_plane, 1, 2, 4)
     for p in ORDER[1:]:
         keys.arrive(p)
-        run(forward, keys, (previous,))
-        previous = p
-    run(forward, keys, (previous,))
-
-    def diagonal(a):
-        return jnp.where(left, a[0:T], a[T : 2 * T])
-
-    stats = jnp.zeros((T, T), F32)
+    plane_keys.arrive(3)
+    plane_keys.arrive(5)
+    run_plane(forward_plane, 3, 5)
+    run(forward, keys, ORDER)
 
     def put(stats, i, column):
         return jnp.where(lane == i, column, stats)
 
-    for i in range(2):
-        inv = 1.0 / oacc[i, :, T : 2 * T]
-        invb[i] = inv
-        pair = diagonal(oacc[i, :, 0:T] * inv).astype(BF16)
-        att[:, T * i : T * (i + 1)] = pair
-        prod = pair.astype(F32) * qg[0:T, 256 + T * i : 256 + T * (i + 1)].astype(F32)
-        first = jnp.sum(jnp.where(left, prod, 0.0), axis=1, keepdims=True)
-        second = jnp.sum(jnp.where(left, 0.0, prod), axis=1, keepdims=True)
-        delb[i, 0:T, :] = jnp.broadcast_to(first, (T, T))
-        delb[i, T : 2 * T, :] = jnp.broadcast_to(second, (T, T))
-        stats = put(stats, 2 * i, inv[0:T])
-        stats = put(stats, 2 * i + 1, inv[T : 2 * T])
-        stats = put(stats, 5 + 2 * i, first)
-        stats = put(stats, 6 + 2 * i, second)
+    stats = jnp.zeros((T, T), F32)
+    invm[...] = 1.0 / om[:, T : 2 * T]
+    attm = []
+    for i in range(4):
+        part = slice(T * i, T * (i + 1))
+        own = (om[part, 0:T] * invm[part, :]).astype(BF16)
+        attm.append(own)
+        prod = own.astype(F32) * qgm[part, :].astype(F32)
+        delta = jnp.sum(jnp.where(left, 0.0, prod), axis=1, keepdims=True)
+        delm[part, :] = jnp.broadcast_to(delta, (T, T))
+        stats = put(stats, i, invm[part, :])
+        stats = put(stats, 4 + i, delta)
     inv = 1.0 / o4acc[:, T : 2 * T]
     inv4[...] = inv
     last = (o4acc[:, 0:T] * inv).astype(BF16)
     att[:, 256:320] = last[:, D:T]
-    prod = last.astype(F32) * qg[0:T, 512:640].astype(F32)
-    first = jnp.sum(jnp.where(left, 0.0, prod), axis=1, keepdims=True)
-    del4[...] = jnp.broadcast_to(first, (T, T))
-    stats = put(stats, 4, inv)
-    stats = put(stats, 9, first)
-    st[0, 0] = jnp.transpose(stats)[0:16, :]
-    st[0, 0, 10:11, 0:64] = adj
+    prod = last.astype(F32) * qg[0:T, :].astype(F32)
+    delta = jnp.sum(jnp.where(left, 0.0, prod), axis=1, keepdims=True)
+    del4[...] = jnp.broadcast_to(delta, (T, T))
+    stats = put(stats, 16, inv)
+    stats = put(stats, 17, delta)
+    stats = jnp.transpose(stats)
+    stm[0, 0:8, :] = stats[0:8, :]
+    stm[0, 8:16, :] = jnp.concatenate([rows4, rows4], axis=0)
+    st[0, 0] = stats[16:32, :]
+    st[0, 0, 10:11, :] = row
+
+    def stm_copy(i):
+        dev, src, into = (
+            (sibling, 0, slice(1, 2)), (z_peer(1), 0, slice(2, 4)), (z_peer(7), 0, slice(4, 6))
+        )[i]
+        src = slice(0, into.stop - into.start)
+        return remote(stm.at[src], stm.at[into], stmsems.at[0, i], stmsems.at[1, i], dev)
 
     def stb_copy():
         return remote(st.at[0, 0], st.at[0, 1], stsend.at[0], strecv.at[0], sibling)
@@ -307,41 +404,65 @@
             st.at[0], st.at[p], stsend.at[p], strecv.at[p], at(chip - step(p, sgn), core)
         )
 
+    stm_copy(0).start()
     stb_copy().start()
+
+    def wide(a, n):
+        return a if n == T else jnp.concatenate([a, a], axis=1)
+
+    def backward_q(p, n):
+        kv4 = block(kv, p, n)
+        prob = est4[p, :, 0:n].astype(F32) * wide(inv4[...], n)
+        dl = prob * (mm_nt(a4g[...], kv4) - wide(del4[...], n))
+        dq4[...] += mm(dl.astype(BF16), kv4)
+
+    def backward_q_plane(t):
+        tile = block(kvm, t, 256)
+        prob = estm[t].astype(F32) * wide(invm[...], 256)
+        dl = prob * (mm_nt(agm[...], tile) - wide(delm[...], 256))
+        dqm[...] += mm(dl.astype(BF16), tile)
+
+    run_plane(backward_q_plane, 0)
+    stm_copy(0).wait_recv()
+    for i in (1, 2):
+        stm_copy(i).start()
+    run_plane(backward_q_plane, 1)
     stb_copy().wait_recv()
     for p in ORDER[1:]:
         st_copy(p).start()
-
-    share = mm(att[...], wo[...]).astype(BF16)
-    for h in range(4):
-        losrc[h] = share[:, W * h : W * (h + 1)]
-
-    def lo_copy(o):
+    run_plane(backward_q_plane, 2, 3, 4, 5)
+
+    def ret_copy(k, o):
         return remote(
-            losrc.at[lax.rem(head + o, 4)], lobuf.at[o], losend.at[o], lorecv.at[o], x_peer(o)
+            ret.at[k, lax.rem(y + o, 4)], retbuf.at[k, y],
+            retsems.at[0, k, o], retsems.at[1, k, o], column(o),
         )
 
-    for o in (1, 2, 3):
-        lo_copy(o).start()
-
-    def wide(a, n):
-        return a if n == T else jnp.concatenate([a, a], axis=1)
-
-    def backward_q(p, n):
-        k0, k1, v0, v1, kv4 = block(kv, p, n)
-        for i, (k, v) in enumerate(((k0, v0), (k1, v1))):
-            prob = est[p, i, :, 0:n].astype(F32) * wide(invb[i], n)
-            dl = prob * (mm_nt(ag[i], v) - wide(delb[i], n))
-            dq[i] += mm(dl.astype(BF16), k)
-        prob = est4[p, :, 0:n].astype(F32) * wide(inv4[...], n)
-        dl = prob * (mm_nt(a4g[...], kv4) - wide(del4[...], n))
-        dq4[...] += mm(dl.astype(BF16), kv4)
-
+    def give_back(k, parts):
+        for i in range(4):
+            ret[k, i] = parts[i]
+        for o in (1, 3, 2):
+            ret_copy(k, o).start()
+        retbuf[k, y] = ret[k, y]
+
+    def given_back(k):
+        for o in (1, 2, 3):
+            ret_copy(k, o).wait_recv()
+
+    give_back(
+        0,
+        [
+            jnp.where(left, dqm[T * i : T * (i + 1), :] * 0.125, attm[i].astype(F32)).astype(BF16)
+            for i in range(4)
+        ],
+    )
     run(backward_q, None, ORDER)
-    for i in range(2):
-        gs[0, :, T * i : T * (i + 1)] = (diagonal(dq[i]) * 0.125).astype(BF16)
     gs[0, :, 256:320] = (dq4[:, 0:D] * 0.125).astype(BF16)
-
+    plane_queries.arrive(2)
+    plane_queries.arrive(4)
+    plane_queries.arrive(1)
+    for p in ORDER[1:]:
+        queries.arrive(p)
     class Adapters:
         def __init__(self, which, lgsrc, lgbuf, acc, accb, rsbuf, zbuf, fin, sems):
             self.which, self.lgsrc, self.lgbuf = which, lgsrc, lgbuf
@@ -428,39 +549,41 @@
                     c.wait_send()
 
     late = Adapters((0, 1, 2), *parts)
-    inacc[...] = mm(gs[0], wqkv[0:W, :])
 
     me_lane = lax.broadcasted_iota(jnp.int32, (1, T), 1) == view
 
     def backward_kv(p, n):
-        q0, q1, g0, g1, qg4 = block(qg, p, n)
+        qg4 = block(qg, p, n)
         sides = [st[p, s] for s in range(n // T)]
-        invs, deltas = [], []
-        for s in sides:
-            w = jnp.sum(jnp.where(me_lane, s[10:11, :], 0.0), axis=1, keepdims=True)
-            invs.append(s * w)
-        invs = invs[0] if n == T else jnp.concatenate(invs, axis=1)
-        deltas = sides[0] if n == T else jnp.concatenate(sides, axis=1)
-
-        def weigh(e, h):
-            return e * invs[h : h + 1, :]
-
-        def shift(dp, h):
-            return dp - deltas[5 + h : 6 + h, :]
-
-        for i, (q, g) in enumerate(((q0, g0), (q1, g1))):
-            e = jnp.exp(mm_nt(ak[i], q))
-            dp = mm_nt(av[i], g)
-            prob = [weigh(e[0:T], 2 * i), weigh(e[T : 2 * T], 2 * i + 1)]
-            dl = [prob[0] * shift(dp[0:T], 2 * i), prob[1] * shift(dp[T : 2 * T], 2 * i + 1)]
-            prob = jnp.concatenate(prob, axis=0).astype(BF16)
-            dl = jnp.concatenate(dl, axis=0).astype(BF16)
-            dk[i] += mm(dl, q)
-            dv[i] += mm(prob, g)
+        w = [jnp.sum(jnp.where(me_lane, s[10:11, :], 0.0), axis=1, keepdims=True) for s in sides]
+        w = [jnp.broadcast_to(one, (1, T)) for one in w]
+        w = w[0] if n == T else jnp.concatenate(w, axis=1)
+        sides = sides[0] if n == T else jnp.concatenate(sides, axis=1)
         both = mm_nt(a4kv[...], qg4)
-        prob = weigh(jnp.exp(both[0:T]), 4)
-        dl = prob * shift(both[T : 2 * T], 4)
+        prob = jnp.where(w > 0.0, jnp.exp(both[0:T]) * sides[0:1, :], 0.0)
+        dl = prob * (both[T : 2 * T] - sides[1:2, :])
         dkv4[...] += mm(jnp.concatenate([dl, prob], axis=0).astype(BF16), qg4)
+
+    mine4 = z * 8 + 2 * sub4 + core
+
+    def mask_kv(g):
+        for i in range(4):
+            line = jnp.broadcast_to(stm[g, 8 + i : 9 + i, :], (4, T))
+            one = jnp.sum(jnp.where(lane4 == mine4, line, 0.0), axis=1, keepdims=True)
+            wk[2 * g + i // 2, 0:4, T * (i % 2) : T * (i % 2 + 1)] = jnp.broadcast_to(one, (4, T))
+
+    def backward_kv_plane(g):
+        mask_kv(g)
+        for half in range(2):
+            t = 2 * g + half
+            tile = block(qgm, t, 256)
+            i = 2 * half
+            inv = jnp.concatenate([stm[g, i : i + 1, :], stm[g, i + 1 : i + 2, :]], axis=1)
+            delta = jnp.concatenate([stm[g, 4 + i : 5 + i, :], stm[g, 5 + i : 6 + i, :]], axis=1)
+            prob = masked(wk[t], jnp.exp(mm_nt(akm[...], tile)) * inv)
+            dl = prob * (mm_nt(avm[...], tile) - delta)
+            dkm[...] += mm(dl.astype(BF16), tile)
+            dvm[...] += mm(prob.astype(BF16), tile)
 
     def run_kv(*order):
         for p in order:
@@ -468,13 +591,38 @@
                 st_copy(p).wait_recv()
         run(backward_kv, queries, order)
 
-    queries.arrive(1, 2, 8, 5, 6, 7, 3, 4)
+    backward_kv_plane(0)
+    backward_kv_plane(1)
+    for i in (1, 2):
+        stm_copy(i).wait_recv()
+    backward_kv_plane(2)
+    backward_kv_plane(4)
+    plane_queries.arrive(3)
+    plane_queries.arrive(5)
+    backward_kv_plane(3)
+    backward_kv_plane(5)
+    give_back(
+        1,
+        [
+            jnp.where(left, dkm[T * i : T * (i + 1), :] * 0.125, dvm[T * i : T * (i + 1), :]).astype(
+                BF16
+            )
+            for i in range(4)
+        ],
+    )
     run_kv(*ORDER)
-    for i in range(2):
-        gs[1, :, T * i : T * (i + 1)] = (diagonal(dk[i]) * 0.125).astype(BF16)
-        gs[2, :, T * i : T * (i + 1)] = diagonal(dv[i]).astype(BF16)
+    given_back(0)
+    for h in range(4):
+        gs[0, :, D * h : D * (h + 1)] = retbuf[0, h, :, 0:D]
+        att[:, D * h : D * (h + 1)] = retbuf[0, h, :, D:T]
+
+    inacc[...] = mm(gs[0], wqkv[0:W, :])
     gs[1, :, 256:320] = (dkv4[0:T, 0:D] * 0.125).astype(BF16)
     gs[2, :, 256:320] = dkv4[T : 2 * T, D:T].astype(BF16)
+    given_back(1)
+    for h in range(4):
+        gs[1, :, D * h : D * (h + 1)] = retbuf[1, h, :, 0:D]
+        gs[2, :, D * h : D * (h + 1)] = retbuf[1, h, :, D:T]
 
     late.send_low()
 
@@ -490,7 +638,21 @@
 
     for o in (1, 2, 3):
         gi_copy(o).start()
+
+    share = mm(att[...], wo[...]).astype(BF16)
+    for h in range(4):
+        losrc[h] = share[:, W * h : W * (h + 1)]
+
+    def lo_copy(o):
+        return remote(
+            losrc.at[lax.rem(head + o, 4)], lobuf.at[o], losend.at[o], lorecv.at[o], x_peer(o)
+        )
+
+    for o in (1, 2, 3):
+        lo_copy(o).start()
     late.send_plane()
+
+    late.send_z()
 
     own = gisrc[head].astype(F32)
     for o in (1, 2, 3):
@@ -503,7 +665,6 @@
         out = out + lobuf[o].astype(F32)
     lo_ref[0] = jnp.transpose(out).astype(BF16)
 
-    late.send_z()
     late.send_back()
     late.finish()
 
@@ -514,6 +675,14 @@
         gi_copy(o).wait_send()
     keys.drain()
     queries.drain()
+    plane_keys.drain()
+    plane_queries.drain()
+    for o in (1, 2, 3):
+        adj_copy(o).wait_send()
+        ret_copy(0, o).wait_send()
+        ret_copy(1, o).wait_send()
+    for i in range(3):
+        stm_copy(i).wait_send()
 
     stb_copy().wait_send()
     for p in ORDER[1:]:
@@ -542,16 +711,20 @@
         vmem((3 * R, W), BF16), dma((6,)),
         vmem((1280, T), BF16), vmem((1280, T), BF16), vmem((3, W, R), BF16),
         vmem((1280, 3 * R), BF16), dma((4,)), dma((4,)), dma((4,)), dma((4,)),
-        vmem((17 * T, 640), BF16), vmem((17 * T, 640), BF16),
+        vmem((4, T, T), BF16), vmem((4, T, T), BF16), vmem((24 * T, T), BF16),
+        vmem((24 * T, T), BF16), dma((2, 10)), dma((2, 10)), vmem((4, 8, T), F32), dma((2, 4)),
+        vmem((6, 16, T), F32), dma((2, 3)), vmem((2, 4, T, T), BF16), vmem((2, 4, T, T), BF16),
+        dma((2, 2, 4)),
+        vmem((512, T), BF16), vmem((512, T), BF16), vmem((512, T), BF16), vmem((512, T), BF16),
+        vmem((12, 8, 256), F32), vmem((12, 8, 256), F32), vmem((12, 512, 256), BF16),
+        vmem((512, 256), F32), vmem((512, T), F32), vmem((512, T), F32), vmem((512, T), F32),
+        vmem((512, T), F32), vmem((512, T), F32),
+        vmem((17 * T, T), BF16), vmem((17 * T, T), BF16),
         dma((9,)), dma((9,)), dma((8,)), dma((8,)), dma((9,)), dma((9,)), dma((8,)), dma((8,)),
         vmem((9, 2, 16, T), F32), dma((9,)), dma((9,)),
-        vmem((2, 256, T), BF16), vmem((2, 256, T), BF16), vmem((T, T), BF16), vmem((T, T), BF16),
-        vmem((2, 256, T), BF16), vmem((2, 256, T), BF16), vmem((256, T), BF16),
-        vmem((16, 256), F32),
-        vmem((9, 2, 256, 256), BF16), vmem((9, T, 256), BF16), vmem((2, 256, 256), F32),
-        vmem((T, 256), F32), vmem((2, 256, T), F32), vmem((2, 256, T), F32), vmem((T, T), F32),
-        vmem((T, T), F32), vmem((2, 256, T), F32), vmem((T, T), F32), vmem((2, 256, T), F32),
-        vmem((2, 256, T), F32), vmem((256, T), F32),
+        vmem((T, T), BF16), vmem((T, T), BF16), vmem((256, T), BF16), vmem((16, 256), F32),
+        vmem((9, T, 256), BF16), vmem((T, 256), F32), vmem((T, T), F32), vmem((T, T), F32),
+        vmem((T, T), F32), vmem((256, T), F32),
         vmem((T, W), BF16), vmem((3, T, W), BF16), vmem((3 * R, T), BF16), vmem((T, 1280), F32),
         vmem((4, T, W), BF16), vmem((4, T, W), BF16), dma((4,)), dma((4,)),
         vmem((4, T, W), BF16), vmem((4, T, W), BF16), dma((4,)), dma((4,)), vmem((3 * R, T), BF16),

time: 89.5 us -> 81.4 us (0.909)
  Pallas kernels: 88.8 us -> 80.5 us
    pallas_call x1, Pallas kernels: 86.9 us -> 78.6 us  [body(): pl.pallas_call(kernel, out_shape=(jax.ShapeDtypeStruct((1, W, T), BF16),...]
where the time goes in v2:
time: 81.4 us; the launch traced here: 81.3 us
  Pallas kernels  80.5 us (99%)
    pallas_call x1, Pallas kernels, body(): pl.pallas_call(kernel, out_shape=(jax.ShapeDtypeStruct((1, W, T), BF16),...  78.6 us
    pallas_call x1, Pallas kernels, body(): pl.pallas_call(hand_over, out_shape=tuple((jax.ShapeDtypeStruct(r.shape,...  1.93 us

profile of v2, /device:TPU:1, one launch (start us, length us, event | category | flops | bytes accessed | tf_op | source)
XLA Modules:
  0.0 81.3 jit_solution(14019253124179767372)
XLA Ops:
  0.6 78.6 %layer.1 = (bf16[1,320,128]{2,1,0:T(8,128)(2,1)}, bf16[1,320,128]{2,1,0:T(8,128)(2,1)}, f32[3,64,320]{2,1,0:T(8,128)}, f32[3,64,320]{2,1,0:T(8,128)}) custom-call(s32[1,64]{1,0:T(1,128)} %adj_ref.1, bf16[1,320,128]{2,1,0:T(8,128)(2,1)} %bitcast.15, bf16[1,320,128]{2,1,0:T(8,128)(2,1)} %bitcast.16, bf16[960,1280]{1,0:T(8,128)(2,1)} %bitcast.12, ...), custom_call_target="tpu_custom_call" | custom-call | tf_op jit(solution)/shard_map/layer/pallas_call | solution.py:737
  79.2 1.9 %hand_over.1 = (bf16[1,320,128]{2,1,0:T(8,128)(2,1)}, bf16[1,320,128]{2,1,0:T(8,128)(2,1)}, f32[3,64,320]{2,1,0:T(8,128)}, f32[3,64,320]{2,1,0:T(8,128)}) custom-call(bf16[1,320,128]{2,1,0:T(8,128)(2,1)} %get-tuple-element.12.refs_0_, bf16[1,320,128]{2,1,0:T(8,128)(2,1)} %get-tuple-element.13.refs_1_, f32[3,64,320]{2,1,0:T(8,128)} %get-tuple-element.14.refs_2_, ...), custom_call_target="tpu_custom_call" | custom-call | tf_op jit(solution)/shard_map/hand_over/pallas_call | solution.py:761

commit v3 on v2

--- a/solution.py
+++ b/solution.py
@@ -29,7 +29,7 @@
     lo_ref, gi_ref, ga_ref, gb_ref,
     wqkv, wo, down, up, wsem,
     xt, ogt, upt, downn, xsend, xrecv, ogsend, ogrecv,
-    kvo, qgo, kvm, qgm, kvmsems, qgmsems, adjq, adjsems, stm, stmsems, ret, retbuf, retsems,
+    kvo, qo, go, qsw, q4, kvosems, qosems, gosems, kvm, qgm, kvmsems, qgmsems, adjq, adjsems, stm, stmsems, ret, retbuf, retsems,
     aqm, agm, akm, avm, wq, wk, estm, om, invm, delm, dqm, dkm, dvm,
     kv, qg, kvsend, kvrecv, kvbsend, kvbrecv, qgsend, qgrecv, qgbsend, qgbrecv,
     st, stsend, strecv,
@@ -60,9 +60,6 @@
     def z_peer(o):
         return (lax.rem(z + o, 8) * 8 + spot, head)
 
-    def spot_peer(o):
-        return (z * 8 + lax.rem(spot + o, 8), head)
-
     def x_peer(o):
         return (view, lax.rem(head + o, 4))
 
@@ -82,8 +79,7 @@
             )
         )
     ]
-    for load in loads:
-        load.start()
+    loads[0].start()
 
     barrier = pltpu.get_barrier_semaphore()
 
@@ -110,6 +106,8 @@
 
     for o in (1, 3, 2):
         x_copy(o).start()
+    for load in loads[1:]:
+        load.start()
 
     adj = adj_ref[...].astype(F32)
     lane64 = lax.broadcasted_iota(jnp.int32, (1, 64), 1)
@@ -216,35 +214,44 @@
     def span(group):
         return slice(512 * group, 512 * (group + 1))
 
-    class Planes:
+    class Swap:
         def __init__(self, out, buf, sems):
             self.out, self.buf, self.sems = out, buf, sems
-
-        def swap(self, o):
+            self.rows = pl.ds(pl.multiple_of(y * T, T), T)
+
+        def copy(self, o):
             return remote(
-                self.out.at[lax.rem(y + o, 4)], self.buf.at[pl.ds(pl.multiple_of(y * T, T), T)],
+                self.out.at[lax.rem(y + o, 4)], self.buf.at[self.rows],
                 self.sems.at[0, o], self.sems.at[1, o], column(o),
             )
 
-        def group(self, src, into, dev):
+        def start(self):
+            for o in (1, 3, 2):
+                self.copy(o).start()
+            self.buf[self.rows, :] = self.out[y]
+
+        def arrived(self):
+            for o in (1, 3, 2):
+                self.copy(o).wait_recv()
+
+        def drain(self):
+            for o in (1, 2, 3):
+                self.copy(o).wait_send()
+
+    class Planes:
+        def __init__(self, buf, sems):
+            self.buf, self.sems = buf, sems
+
+        def move(self, into):
+            src, dev = into - 1, sibling
+            if into in (2, 4):
+                src, dev = 0, z_peer(1 if into == 2 else 7)
             return remote(
                 self.buf.at[span(src)], self.buf.at[span(into)],
-                self.sems.at[0, 4 + into], self.sems.at[1, 4 + into], dev,
+                self.sems.at[0, into], self.sems.at[1, into], dev,
             )
 
-        def move(self, into):
-            if into in (2, 4):
-                return self.group(0, into, z_peer(1 if into == 2 else 7))
-            return self.group(into - 1, into, sibling)
-
         def start(self):
-            for o in (1, 3, 2):
-                self.swap(o).start()
-            self.buf[pl.ds(pl.multiple_of(y * T, T), T), :] = self.out[y]
-
-        def swapped(self):
-            for o in (1, 3, 2):
-                self.swap(o).wait_recv()
             for g in (2, 4, 1):
                 self.move(g).start()
 
@@ -254,25 +261,31 @@
                 self.move(group + 1).start()
 
         def drain(self):
-            for o in (1, 2, 3):
-                self.swap(o).wait_send()
             for g in range(1, 6):
                 self.move(g).wait_send()
 
-    plane_keys = Planes(kvo, kvm, kvmsems)
-    plane_queries = Planes(qgo, qgm, qgmsems)
+    swaps = [Swap(kvo, kvm, kvosems), Swap(qo, qsw, qosems), Swap(go, agm, gosems)]
+    plane_keys = Planes(kvm, kvmsems)
+    plane_queries = Planes(qgm, qgmsems)
     keys = Blocks(kv, kvsend, kvrecv, kvbsend, kvbrecv)
     queries = Blocks(qg, qgsend, qgrecv, qgbsend, qgbrecv)
+    swaps[0].start()
+
+    def spread(out, last, parts):
+        for h in range(5):
+            tile = jnp.transpose(jnp.concatenate(parts(slice(D * h, D * (h + 1))), axis=0))
+            if h < 4:
+                out[h] = tile
+            else:
+                last[...] = tile
+
+    nothing = jnp.zeros((D, T), BF16)
+    query = project(0)
+    spread(qo, q4, lambda part: [query[part], nothing])
+    swaps[1].start()
+    swaps[0].arrived()
     plane_keys.start()
-    query = project(0)
-    plane_keys.swapped()
     keys.start_own()
-    loads[5].wait()
-    loads[4].wait()
-    for o in (1, 2, 3):
-        og_copy(o).wait_recv()
-    lay_out(qgo, qg, query, mm(wo[...], ogt[...]).astype(BF16))
-    plane_queries.start()
 
     for o in (1, 2, 3):
         adj_copy(o).wait_recv()
@@ -289,27 +302,27 @@
             one = jnp.sum(jnp.where(lane4 == view_of(g, i), rows4, 0.0), axis=1, keepdims=True)
             wq[2 * g + i // 2, 0:4, T * (i % 2) : T * (i % 2 + 1)] = jnp.broadcast_to(one, (4, T))
 
-    plane_queries.swapped()
-    queries.start_own()
-
-    def tall(a, n):
-        return jnp.concatenate([a] * n, axis=0)
-
     eighth = jnp.asarray(0.125, BF16)
-    tile = qg[0:T, :]
-    a4q[...] = jnp.where(left, tile * eighth, jnp.zeros_like(tile))
-    a4g[...] = jnp.where(left, jnp.zeros_like(tile), tile)
+    swaps[1].arrived()
+    a4q[...] = q4[...] * eighth
     tile = kv[0:T, :]
     a4kv[0:T, :] = jnp.where(left, tile * eighth, jnp.zeros_like(tile))
     a4kv[T : 2 * T, :] = jnp.where(left, jnp.zeros_like(tile), tile)
-    for i in range(4):
-        part = slice(T * i, T * (i + 1))
-        tile = qgm[part, :]
-        aqm[part, :] = jnp.where(left, tile * eighth, jnp.zeros_like(tile))
-        agm[part, :] = jnp.where(left, jnp.zeros_like(tile), tile)
+    quarters = [slice(T * i, T * (i + 1)) for i in range(4)]
+    for part in quarters:
+        aqm[part, :] = qsw[part, :] * eighth
         tile = kvm[part, :]
         akm[part, :] = jnp.where(left, tile * eighth, jnp.zeros_like(tile))
         avm[part, :] = jnp.where(left, jnp.zeros_like(tile), tile)
+
+    loads[5].wait()
+    loads[4].wait()
+    for o in (1, 2, 3):
+        og_copy(o).wait_recv()
+    grad_att = mm(wo[...], ogt[...]).astype(BF16)
+    spread(go, a4g, lambda part: [nothing, grad_att[part]])
+    swaps[2].start()
+    qg[0:T, :] = jnp.where(left, q4[...], a4g[...])
 
     for ref in (om, dqm, dkm, dvm, o4acc, dq4, dkv4):
         ref[...] = jnp.zeros_like(ref)
@@ -348,6 +361,11 @@
             pl.loop(2 * g, 2 * g + 2)(work)
 
     run_plane(forward_plane, 0)
+    swaps[2].arrived()
+    for part in quarters:
+        qgm[part, :] = jnp.where(left, qsw[part, :], agm[part, :])
+    plane_queries.start()
+    queries.start_own()
     plane_keys.arrive(2)
     plane_keys.arrive(4)
     plane_keys.arrive(1)
@@ -464,30 +482,40 @@
     for p in ORDER[1:]:
         queries.arrive(p)
     class Adapters:
-        def __init__(self, which, lgsrc, lgbuf, acc, accb, rsbuf, zbuf, fin, sems):
-            self.which, self.lgsrc, self.lgbuf = which, lgsrc, lgbuf
-            self.acc, self.accb, self.rsbuf, self.zbuf, self.fin = acc, accb, rsbuf, zbuf, fin
-            self.sems = sems
+        def __init__(
+            self, which, lgsrc, lgbuf, acc, accb, other, half, halfb, rsbuf, zbuf, fin, sems
+        ):
+            self.which, self.lgsrc, self.lgbuf, self.acc, self.accb = which, lgsrc, lgbuf, acc, accb
+            self.other, self.half, self.halfb = other, half, halfb
+            self.rsbuf, self.zbuf, self.fin, self.sems = rsbuf, zbuf, fin, sems
             self.count = R * len(which)
             self.share = self.count // 4
+            self.spot = core * 4 + y
 
         def part(self, i):
             return pl.ds(pl.multiple_of(i * self.share, 16), self.share)
+
+        def core_rows(self, k):
+            return pl.ds(pl.multiple_of(k * self.count, 64), self.count)
 
         def copies(self, stage):
             def copy(o):
                 ends = {
                     0: lambda: (self.lgsrc, self.lgbuf.at[o], x_peer(o)),
-                    1: lambda: (
-                        self.accb.at[self.part(lax.rem(spot + o, 8))], self.rsbuf.at[o], spot_peer(o)
+                    1: lambda: (self.accb.at[self.core_rows(1 - core)], self.other, sibling),
+                    2: lambda: (
+                        self.halfb.at[self.part(lax.rem(y + o, 4))], self.rsbuf.at[o], column(o)
                     ),
-                    2: lambda: (self.zbuf.at[z], self.zbuf.at[z], z_peer(o)),
-                    3: lambda: (self.fin.at[spot], self.fin.at[spot], spot_peer(o)),
+                    3: lambda: (self.zbuf.at[z], self.zbuf.at[z], z_peer(o)),
+                    4: lambda: (self.fin.at[self.spot], self.fin.at[self.spot], column(o)),
+                    5: lambda: (
+                        self.fin.at[pl.ds(4 * core, 4)], self.fin.at[pl.ds(4 * core, 4)], sibling
+                    ),
                 }
                 src, dst, dev = ends[stage]()
                 return remote(src, dst, self.sems.at[stage, 0, o], self.sems.at[stage, 1, o], dev)
 
-            return [copy(o) for o in range(1, 8 if stage else 4)]
+            return [copy(o) for o in range(1, (4, 2, 4, 8, 4, 2)[stage])]
 
         def start(self, stage):
             for c in self.copies(stage):
@@ -518,24 +546,32 @@
             self.accb[...] = self.acc[...].astype(BF16)
             self.start(1)
 
+        def send_column(self):
+            self.wait(1)
+            self.half[...] = self.acc[self.core_rows(core), :] + self.other[...].astype(F32)
+            self.halfb[...] = self.half[...].astype(BF16)
+            self.start(2)
+
         def send_z(self):
-            self.wait(1)
-            total = self.acc[self.part(spot), :]
-            for o in range(1, 8):
+            self.wait(2)
+            total = self.half[self.part(y), :]
+            for o in range(1, 4):
                 total = total + self.rsbuf[o].astype(F32)
             self.zbuf[z] = total.astype(BF16)
-            self.start(2)
+            self.start(3)
 
         def send_back(self):
-            self.wait(2)
+            self.wait(3)
             total = self.zbuf[0].astype(F32)
             for i in range(1, 8):
                 total = total + self.zbuf[i].astype(F32)
-            self.fin[spot] = total.astype(BF16)
-            self.start(3)
+            self.fin[self.spot] = total.astype(BF16)
+            self.start(4)
 
         def finish(self):
-            self.wait(3)
+            self.wait(4)
+            self.start(5)
+            self.wait(5)
             for i in range(8):
                 for r in range(0, self.share, 16):
                     which, at_row = divmod((i % 4) * self.share + r, R)
@@ -544,11 +580,12 @@
                     out[self.which[which], rows, :] = self.fin[i, r : r + 16, :].astype(F32)
 
         def drain(self):
-            for stage in range(4):
+            for stage in range(6):
                 for c in self.copies(stage):
                     c.wait_send()
 
-    late = Adapters((0, 1, 2), *parts)
+    early = Adapters((0,), *parts[:11])
+    late = Adapters((1, 2), *parts[11:])
 
     me_lane = lax.broadcasted_iota(jnp.int32, (1, T), 1) == view
 
@@ -616,6 +653,7 @@
         gs[0, :, D * h : D * (h + 1)] = retbuf[0, h, :, 0:D]
         att[:, D * h : D * (h + 1)] = retbuf[0, h, :, D:T]
 
+    early.send_low()
     inacc[...] = mm(gs[0], wqkv[0:W, :])
     gs[1, :, 256:320] = (dkv4[0:T, 0:D] * 0.125).astype(BF16)
     gs[2, :, 256:320] = dkv4[T : 2 * T, D:T].astype(BF16)
@@ -625,6 +663,7 @@
         gs[2, :, D * h : D * (h + 1)] = retbuf[1, h, :, D:T]
 
     late.send_low()
+    early.send_plane()
 
     share = inacc[...] + mm(gs[1], wqkv[W : 2 * W, :]) + mm(gs[2], wqkv[2 * W : 3 * W, :])
     share = share.astype(BF16)
@@ -650,8 +689,10 @@
 
     for o in (1, 2, 3):
         lo_copy(o).start()
+    early.send_column()
     late.send_plane()
-
+    early.send_z()
+    late.send_column()
     late.send_z()
 
     own = gisrc[head].astype(F32)
@@ -665,7 +706,9 @@
         out = out + lobuf[o].astype(F32)
     lo_ref[0] = jnp.transpose(out).astype(BF16)
 
+    early.send_back()
     late.send_back()
+    early.finish()
     late.finish()
 
     for o in (1, 2, 3):
@@ -677,6 +720,8 @@
     queries.drain()
     plane_keys.drain()
     plane_queries.drain()
+    for swap in swaps:
+        swap.drain()
     for o in (1, 2, 3):
         adj_copy(o).wait_send()
         ret_copy(0, o).wait_send()
@@ -687,6 +732,7 @@
     stb_copy().wait_send()
     for p in ORDER[1:]:
         st_copy(p).wait_send()
+    early.drain()
     late.drain()
 
 
@@ -711,8 +757,9 @@
         vmem((3 * R, W), BF16), dma((6,)),
         vmem((1280, T), BF16), vmem((1280, T), BF16), vmem((3, W, R), BF16),
         vmem((1280, 3 * R), BF16), dma((4,)), dma((4,)), dma((4,)), dma((4,)),
-        vmem((4, T, T), BF16), vmem((4, T, T), BF16), vmem((24 * T, T), BF16),
-        vmem((24 * T, T), BF16), dma((2, 10)), dma((2, 10)), vmem((4, 8, T), F32), dma((2, 4)),
+        vmem((4, T, T), BF16), vmem((4, T, T), BF16), vmem((4, T, T), BF16), vmem((512, T), BF16),
+        vmem((T, T), BF16), dma((2, 4)), dma((2, 4)), dma((2, 4)), vmem((24 * T, T), BF16),
+        vmem((24 * T, T), BF16), dma((2, 6)), dma((2, 6)), vmem((4, 8, T), F32), dma((2, 4)),
         vmem((6, 16, T), F32), dma((2, 3)), vmem((2, 4, T, T), BF16), vmem((2, 4, T, T), BF16),
         dma((2, 2, 4)),
         vmem((512, T), BF16), vmem((512, T), BF16), vmem((512, T), BF16), vmem((512, T), BF16),
@@ -729,9 +776,11 @@
         vmem((4, T, W), BF16), vmem((4, T, W), BF16), dma((4,)), dma((4,)),
         vmem((4, T, W), BF16), vmem((4, T, W), BF16), dma((4,)), dma((4,)), vmem((3 * R, T), BF16),
     ]
-    share = vmem((8, 6 * R // 8, W), BF16)
-    scratch += [vmem((3 * R, T), BF16), vmem((4, 3 * R, T), BF16), vmem((6 * R, W), F32)]
-    scratch += [vmem((6 * R, W), BF16), share, share, share, dma((4, 2, 8))]
+    for count in (R, 2 * R):
+        share, half = vmem((8, count // 4, W), BF16), vmem((count, W), BF16)
+        scratch += [vmem((count, T), BF16), vmem((4, count, T), BF16), vmem((2 * count, W), F32)]
+        scratch += [vmem((2 * count, W), BF16), half, vmem((count, W), F32), half]
+        scratch += [share, share, share, dma((6, 2, 8))]
     whole = pl.BlockSpec(memory_space=pltpu.VMEM)
     hbm = pl.BlockSpec(memory_space=pltpu.HBM)
     results = pl.pallas_call(

time: 81.4 us -> 78.9 us (0.969)
  Pallas kernels: 80.5 us -> 78 us
    pallas_call x1, Pallas kernels: 78.6 us -> 76.1 us  [body(): pl.pallas_call(kernel, out_shape=(jax.ShapeDtypeStruct((1, W, T), BF16),...]
where the time goes in v3:
time: 78.9 us; the launch traced here: 78.8 us
  Pallas kernels  78 us (99%)
  between operations  0.8 us (1%)
    pallas_call x1, Pallas kernels, body(): pl.pallas_call(kernel, out_shape=(jax.ShapeDtypeStruct((1, W, T), BF16),...  76.1 us
    pallas_call x1, Pallas kernels, body(): pl.pallas_call(hand_over, out_shape=tuple((jax.ShapeDtypeStruct(r.shape,...  1.93 us

profile of v3, /device:TPU:1, one launch (start us, length us, event | category | flops | bytes accessed | tf_op | source)
XLA Modules:
  0.0 78.8 jit_solution(2581579673627040445)
XLA Ops:
  0.6 76.1 %layer.1 = (bf16[1,320,128]{2,1,0:T(8,128)(2,1)}, bf16[1,320,128]{2,1,0:T(8,128)(2,1)}, f32[3,64,320]{2,1,0:T(8,128)}, f32[3,64,320]{2,1,0:T(8,128)}) custom-call(s32[1,64]{1,0:T(1,128)} %adj_ref.1, bf16[1,320,128]{2,1,0:T(8,128)(2,1)} %bitcast.15, bf16[1,320,128]{2,1,0:T(8,128)(2,1)} %bitcast.16, bf16[960,1280]{1,0:T(8,128)(2,1)} %bitcast.12, ...), custom_call_target="tpu_custom_call" | custom-call | tf_op jit(solution)/shard_map/layer/pallas_call | solution.py:786
  76.7 1.9 %hand_over.1 = (bf16[1,320,128]{2,1,0:T(8,128)(2,1)}, bf16[1,320,128]{2,1,0:T(8,128)(2,1)}, f32[3,64,320]{2,1,0:T(8,128)}, f32[3,64,320]{2,1,0:T(8,128)}) custom-call(bf16[1,320,128]{2,1,0:T(8,128)(2,1)} %get-tuple-element.12.refs_0_, bf16[1,320,128]{2,1,0:T(8,128)(2,1)} %get-tuple-element.13.refs_1_, f32[3,64,320]{2,1,0:T(8,128)} %get-tuple-element.14.refs_2_, ...), custom_call_target="tpu_custom_call" | custom-call | tf_op jit(solution)/shard_map/hand_over/pallas_call | solution.py:810

commit v4 on v3

--- a/solution.py
+++ b/solution.py
@@ -12,7 +12,7 @@
 W = 320
 D = 64
 R = 64
-ORDER = (0, 1, 2, 8, 5, 6, 7, 3, 4)
+ORDER = (0, 3, 4, 1, 2, 5, 6, 8, 7)
 CHIPS = 32
 
 
@@ -104,7 +104,7 @@
     def og_copy(o):
         return remote(og_hbm.at[0], ogt.at[mine], ogsend.at[o], ogrecv.at[o], x_peer(o))
 
-    for o in (1, 3, 2):
+    for o in (2, 1, 3):
         x_copy(o).start()
     for load in loads[1:]:
         load.start()
@@ -132,7 +132,7 @@
     def adj_copy(o):
         return remote(adjq.at[y], adjq.at[y], adjsems.at[0, o], adjsems.at[1, o], column(o))
 
-    for o in (1, 3, 2):
+    for o in (2, 1, 3):
         adj_copy(o).start()
 
     for load in loads[1:3]:
@@ -146,7 +146,7 @@
     loads[0].wait()
     for o in (1, 2, 3):
         x_copy(o).wait_recv()
-    for o in (1, 3, 2):
+    for o in (2, 1, 3):
         og_copy(o).start()
     low[...] = mm(down[...], xt[...]).astype(BF16)
 
@@ -226,12 +226,12 @@
             )
 
         def start(self):
-            for o in (1, 3, 2):
+            for o in (2, 1, 3):
                 self.copy(o).start()
             self.buf[self.rows, :] = self.out[y]
 
         def arrived(self):
-            for o in (1, 3, 2):
+            for o in (2, 1, 3):
                 self.copy(o).wait_recv()
 
         def drain(self):
@@ -459,7 +459,7 @@
     def give_back(k, parts):
         for i in range(4):
             ret[k, i] = parts[i]
-        for o in (1, 3, 2):
+        for o in (2, 1, 3):
             ret_copy(k, o).start()
         retbuf[k, y] = ret[k, y]
 
@@ -515,7 +515,8 @@
                 src, dst, dev = ends[stage]()
                 return remote(src, dst, self.sems.at[stage, 0, o], self.sems.at[stage, 1, o], dev)
 
-            return [copy(o) for o in range(1, (4, 2, 4, 8, 4, 2)[stage])]
+            far = {1: (1,), 3: (4, 3, 5, 2, 6, 1, 7), 5: (1,)}
+            return [copy(o) for o in far.get(stage, (2, 1, 3))]
 
         def start(self, stage):
             for c in self.copies(stage):
@@ -579,8 +580,8 @@
                     rows = slice(at_row, at_row + 16)
                     out[self.which[which], rows, :] = self.fin[i, r : r + 16, :].astype(F32)
 
-        def drain(self):
-            for stage in range(6):
+        def drain(self, *stages):
+            for stage in stages:
                 for c in self.copies(stage):
                     c.wait_send()
 
@@ -706,11 +707,6 @@
         out = out + lobuf[o].astype(F32)
     lo_ref[0] = jnp.transpose(out).astype(BF16)
 
-    early.send_back()
-    late.send_back()
-    early.finish()
-    late.finish()
-
     for o in (1, 2, 3):
         x_copy(o).wait_send()
         og_copy(o).wait_send()
@@ -732,8 +728,16 @@
     stb_copy().wait_send()
     for p in ORDER[1:]:
         st_copy(p).wait_send()
-    early.drain()
-    late.drain()
+    for part in (early, late):
+        part.drain(0, 1, 2)
+
+    early.send_back()
+    late.send_back()
+    early.finish()
+    late.finish()
+
+    for part in (early, late):
+        part.drain(3, 4, 5)
 
 
 def hand_over(*refs):

time: 78.9 us -> 77.2 us (0.978)
  Pallas kernels: 78 us -> 76.3 us
    pallas_call x1, Pallas kernels: 76.1 us -> 74.3 us  [body(): pl.pallas_call(kernel, out_shape=(jax.ShapeDtypeStruct((1, W, T), BF16),...]
where the time goes in v4:
time: 77.2 us; the launch traced here: 77.1 us
  Pallas kernels  76.3 us (99%)
  between operations  0.8 us (1%)
    pallas_call x1, Pallas kernels, body(): pl.pallas_call(kernel, out_shape=(jax.ShapeDtypeStruct((1, W, T), BF16),...  74.3 us
    pallas_call x1, Pallas kernels, body(): pl.pallas_call(hand_over, out_shape=tuple((jax.ShapeDtypeStruct(r.shape,...  1.93 us

profile of v4, /device:TPU:1, one launch (start us, length us, event | category | flops | bytes accessed | tf_op | source)
XLA Modules:
  0.0 77.1 jit_solution(4102284596926479910)
XLA Ops:
  0.6 74.3 %layer.1 = (bf16[1,320,128]{2,1,0:T(8,128)(2,1)}, bf16[1,320,128]{2,1,0:T(8,128)(2,1)}, f32[3,64,320]{2,1,0:T(8,128)}, f32[3,64,320]{2,1,0:T(8,128)}) custom-call(s32[1,64]{1,0:T(1,128)} %adj_ref.1, bf16[1,320,128]{2,1,0:T(8,128)(2,1)} %bitcast.15, bf16[1,320,128]{2,1,0:T(8,128)(2,1)} %bitcast.16, bf16[960,1280]{1,0:T(8,128)(2,1)} %bitcast.12, ...), custom_call_target="tpu_custom_call" | custom-call | tf_op jit(solution)/shard_map/layer/pallas_call | solution.py:790
  75.0 1.9 %hand_over.1 = (bf16[1,320,128]{2,1,0:T(8,128)(2,1)}, bf16[1,320,128]{2,1,0:T(8,128)(2,1)}, f32[3,64,320]{2,1,0:T(8,128)}, f32[3,64,320]{2,1,0:T(8,128)}) custom-call(bf16[1,320,128]{2,1,0:T(8,128)(2,1)} %get-tuple-element.12.refs_0_, bf16[1,320,128]{2,1,0:T(8,128)(2,1)} %get-tuple-element.13.refs_1_, f32[3,64,320]{2,1,0:T(8,128)} %get-tuple-element.14.refs_2_, ...), custom_call_target="tpu_custom_call" | custom-call | tf_op jit(solution)/shard_map/hand_over/pallas_call | solution.py:814

commit v5 on v4

--- a/solution.py
+++ b/solution.py
@@ -701,6 +701,9 @@
         gi_copy(o).wait_recv()
         own = own + gibuf[o].astype(F32)
     gi_ref[0] = (jnp.transpose(own) + mm(downn[mine, :], lgall[...])).astype(BF16)
+    early.send_back()
+    late.send_back()
+
     out = losrc[head].astype(F32)
     for o in (1, 2, 3):
         lo_copy(o).wait_recv()
@@ -731,8 +734,6 @@
     for part in (early, late):
         part.drain(0, 1, 2)
 
-    early.send_back()
-    late.send_back()
     early.finish()
     late.finish()
 

time: 77.2 us -> 77.2 us (level)
  no operation moved by 1% of the time
where the time goes in v5:
time: 77.2 us; the launch traced here: 77.1 us
  Pallas kernels  76.3 us (99%)
  between operations  0.8 us (1%)
    pallas_call x1, Pallas kernels, body(): pl.pallas_call(kernel, out_shape=(jax.ShapeDtypeStruct((1, W, T), BF16),...  74.3 us
    pallas_call x1, Pallas kernels, body(): pl.pallas_call(hand_over, out_shape=tuple((jax.ShapeDtypeStruct(r.shape,...  1.93 us

profile of v5, /device:TPU:1, one launch (start us, length us, event | category | flops | bytes accessed | tf_op | source)
XLA Modules:
  0.0 77.1 jit_solution(5290014087750456055)
XLA Ops:
  0.6 74.3 %layer.1 = (bf16[1,320,128]{2,1,0:T(8,128)(2,1)}, bf16[1,320,128]{2,1,0:T(8,128)(2,1)}, f32[3,64,320]{2,1,0:T(8,128)}, f32[3,64,320]{2,1,0:T(8,128)}) custom-call(s32[1,64]{1,0:T(1,128)} %adj_ref.1, bf16[1,320,128]{2,1,0:T(8,128)(2,1)} %bitcast.15, bf16[1,320,128]{2,1,0:T(8,128)(2,1)} %bitcast.16, bf16[960,1280]{1,0:T(8,128)(2,1)} %bitcast.12, ...), custom_call_target="tpu_custom_call" | custom-call | tf_op jit(solution)/shard_map/layer/pallas_call | solution.py:791
  75.0 1.9 %hand_over.1 = (bf16[1,320,128]{2,1,0:T(8,128)(2,1)}, bf16[1,320,128]{2,1,0:T(8,128)(2,1)}, f32[3,64,320]{2,1,0:T(8,128)}, f32[3,64,320]{2,1,0:T(8,128)}) custom-call(bf16[1,320,128]{2,1,0:T(8,128)(2,1)} %get-tuple-element.12.refs_0_, bf16[1,320,128]{2,1,0:T(8,128)(2,1)} %get-tuple-element.13.refs_1_, f32[3,64,320]{2,1,0:T(8,128)} %get-tuple-element.14.refs_2_, ...), custom_call_target="tpu_custom_call" | custom-call | tf_op jit(solution)/shard_map/hand_over/pallas_call | solution.py:815
